TPU v7x, 32 devices: a whole 2x2x4 slice. The times are simulated.
32 devices in a mesh: rep: 4 (over y, core), fsdp: 8 (over z, x).
Axes of the slice: x: 2, y: 2, z: 4, core: 2. Of those that a mesh axis runs over, the one named last changes fastest.
Arguments:
- grad: bfloat16 [4, 4096, 8192], P('rep', 'fsdp'), may hold values from -12 to 12
- error: float32 [4, 4096, 8192], P('rep', 'fsdp'), may hold values from -2 to 2
- q_prev: float32 [8192, 32], replicated, may hold values from -6 to 6
Outputs:
- update: bfloat16 [4096, 8192], P('fsdp')
- new_error: float32 [4, 4096, 8192], P('rep', 'fsdp')
- q_next: float32 [8192, 32], replicated
All inputs are finite; a program needn't handle non-finite values.
Results may differ from a plain program's by a relative error of at most 0.001.
Values sent between devices are 32-bit elements; how exact they have to be, the bound alone decides.
No kernel may reach another device: no remote copies, remote signals or barrier semaphores. Data moves between devices by JAX's collectives and lax.ppermute only.
A program may use at most 128 MiB of HBM per device.

v0:
```python
import jax
import jax.numpy as jnp
from jax import lax
from jax.sharding import PartitionSpec as P


def local(grad, error, q_prev):
    highest = lax.Precision.HIGHEST
    replicas = lax.axis_size("rep")
    corrected = grad[0].astype(jnp.float32) + error[0]
    p_part = jnp.dot(corrected, q_prev, precision=highest)
    p_mean = lax.psum(p_part, "rep") / replicas
    gram = lax.psum(jnp.dot(p_mean.T, p_mean, precision=highest), "fsdp")
    rank = gram.shape[0]
    shift = 0.001 * jnp.trace(gram) / rank
    chol = jnp.linalg.cholesky(gram + shift * jnp.eye(rank, dtype=jnp.float32))
    p_hat = lax.linalg.triangular_solve(chol, p_mean, left_side=False, lower=True, transpose_a=True)
    q_terms = jnp.dot(corrected.T, p_hat, precision=highest)
    q_next = lax.psum(q_terms, ("rep", "fsdp")) / replicas
    approx = jnp.dot(p_hat, q_next.T, precision=highest)
    update = approx.astype(jnp.bfloat16)
    new_error = (corrected - approx)[None]
    return (update, new_error, q_next)


def solution(mesh):
    placed = (P("rep", "fsdp", None), P("rep", "fsdp", None), P())
    return jax.shard_map(
        local,
        mesh=mesh,
        in_specs=placed,
        out_specs=(P("fsdp", None), P("rep", "fsdp", None), P()),
        check_vma=False,
    )
```

profile of v0, /device:TPU:1, one launch (start us, length us, event | category | flops | bytes accessed | tf_op | source)
XLA Modules:
  0.0 283.5 jit_solution(13029677510112861701)
XLA Ops:
  7.2 0.0 copy-start
  7.2 0.0 all-reduce.3.cloned.1.call-start
  7.2 1.2 copy-done
  8.4 21.0 %fusion.2 = f32[512,32]{0,1:T(8,128)} fusion(f32[8192,32]{0,1:T(8,128)S(1)} %copy-done, f32[1,512,8192]{2,1,0:T(8,128)} %param.4, bf16[1,512,8192]{2,1,0:T(8,128)(2,1)} %param.3), kind=kOutput, calls=%fused_computation.3 | convolution fusion | flops 1619001344 | bytes 26279936 | tf_op jit(solution)/shard_map/dot_general | solution.py:11
  29.4 0.0 all-reduce.3.cloned.1.call-update
  29.4 0.0 all-reduce.5.cloned.1.call-start
  29.5 31.8 %all-reduce.3.cloned.1.call-done = f32[512,32]{0,1:T(8,128)} async-done(((f32[512,32]{0,1:T(8,128)}), f32[512,32]{0,1:T(8,128)}) %all-reduce.3.cloned.1.call-update) | async-done | bytes 65552 | tf_op jit(solution)/shard_map/psum | solution.py:12
  61.3 1.1 fusion.7
  62.4 30.5 %psum.22 = f32[32,32]{1,0:T(8,128)S(1)} all-reduce(f32[32,32]{1,0:T(8,128)S(1)} %fusion.7), channel_id=1, replica_groups=mesh['rep'=4,'fsdp'=8] {'fsdp'}, use_global_device_ids=true, to_apply=%region_1.0 | all-reduce | flops 1024 | bytes 8192 | tf_op jit(solution)/shard_map/psum | solution.py:13
  92.9 0.6 select_reduce_fusion.1
  94.2 0.1 copy.6
  94.2 2.9 %cholesky.17 = f32[32,32]{1,0:T(8,128)S(1)} custom-call(f32[32,32]{1,0:T(8,128)S(1)} %fusion.13), custom_call_target="Cholesky" | custom-call | tf_op jit(solution)/shard_map/jit(cholesky)/cholesky | solution.py:16
  97.2 0.6 compare_reduce_fusion
  97.8 0.7 fusion.11
  98.5 2.4 custom-call.6
  100.9 1.1 fusion.5
  102.0 16.6 %fusion = f32[8192,32]{0,1:T(8,128)} fusion(f32[512,32]{0,1:T(8,128)S(1)} %fusion.5, f32[1,512,8192]{2,1,0:T(8,128)} %param.4, bf16[1,512,8192]{2,1,0:T(8,128)(2,1)} %param.3), kind=kOutput, calls=%fused_computation.1 | convolution fusion | flops 1619001344 | bytes 26279936 | tf_op jit(solution)/shard_map/dot_general | solution.py:18
  118.6 0.0 all-reduce.5.cloned.1.call-update
  118.6 133.5 %all-reduce.5.cloned.1.call-done = f32[8192,32]{0,1:T(8,128)} async-done(((f32[8192,32]{0,1:T(8,128)}), f32[8192,32]{0,1:T(8,128)}) %all-reduce.5.cloned.1.call-update) | async-done | bytes 1048592 | tf_op jit(solution)/shard_map/psum | solution.py:19
  252.1 1.3 broadcast_multiply_fusion
  253.4 0.0 copy-start.1
  253.4 23.3 %fusion.4 = (f32[1,512,8192]{2,1,0:T(8,128)}, bf16[512,8192]{1,0:T(8,128)(2,1)}) fusion(f32[1,512,8192]{2,1,0:T(8,128)} %param.4, bf16[1,512,8192]{2,1,0:T(8,128)(2,1)} %param.3, f32[512,32]{0,1:T(8,128)S(1)} %fusion.5, f32[8192,32]{0,1:T(8,128)S(1)} %broadcast_multiply_fusion), kind=kOutput, calls=%fused_computation.5 | convolution fusion | flops 1627389952 | bytes 51445760 | tf_op jit(solution)/shard_map/dot_general | solution.py:20
  276.7 0.0 copy-done.1
  (3 shorter events, 0.1 us)
Async XLA Ops:
  7.2 1.2 copy-start
  7.2 54.1 %all-reduce.3.cloned.1.call-start = ((), (), s32[]{:S(2)}) async-start(), calls=%async_computation | async-start | bytes 131072 | tf_op jit(solution)/shard_map/psum | solution.py:12
  29.4 222.7 %all-reduce.5.cloned.1.call-start = ((), (), s32[]{:S(2)}) async-start(), calls=%async_computation.1 | async-start | bytes 2097152 | tf_op jit(solution)/shard_map/psum | solution.py:19
  253.4 23.3 %copy-start.1 = (f32[8192,32]{0,1:T(8,128)}, f32[8192,32]{0,1:T(8,128)S(1)}, u32[]{:S(2)}) copy-start(f32[8192,32]{0,1:T(8,128)S(1)} %broadcast_multiply_fusion) | copy-start | bytes 3145732
Sparse Core Ops, SparseCore 0:
  29.6 31.7 all-reduce.2
  118.7 133.3 all-reduce.4
where the time goes:
time: 285 us; the launch traced here: 284 us
  waiting for transfers between devices  165 us (58%)
  matrix products  63 us (22%)
  blocking collectives  30.5 us (11%)
  between operations  14.7 us (5%)
  other arithmetic  8.6 us (3%)
    psum x1, waiting for transfers between devices, local(): q_next = lax.psum(q_terms, ('rep', 'fsdp')) / replicas  133 us
    psum x1, waiting for transfers between devices, local(): p_mean = lax.psum(p_part, 'rep') / replicas  31.8 us
    psum x1, blocking collectives, local(): gram = lax.psum(jnp.dot(p_mean.T, p_mean, precision=highest), 'fsdp')  30.5 us
    dot_general x1, matrix products, local(): approx = jnp.dot(p_hat, q_next.T, precision=highest)  23.3 us
    dot_general x1, matrix products, local(): p_part = jnp.dot(corrected, q_prev, precision=highest)  21 us
    dot_general x1, matrix products, local(): q_terms = jnp.dot(corrected.T, p_hat, precision=highest)  16.6 us
  transfers between devices with their start and end apart: 2, of which 2 were waited for; matrix products, arithmetic and copies ran while one was open for 0% of the time, Pallas kernels for 0%

commit v1 on v0

v1 whole, which is shorter than its diff:
```python
import functools

import jax
import jax.numpy as jnp
from jax import lax
from jax.experimental import pallas as pl
from jax.experimental.pallas import tpu as pltpu
from jax.sharding import PartitionSpec as P

F32, BF16 = jnp.float32, jnp.bfloat16
HIGHEST = lax.Precision.HIGHEST
AXES = ("rep", "fsdp")
NT = (((1,), (1,)), ((), ()))
NN = (((1,), (0,)), ((), ()))
VMEM = pl.BlockSpec(memory_space=pltpu.VMEM)
PIECES = 32
GRAM_LANES = 128


def params(mib):
    return pltpu.CompilerParams(vmem_limit_bytes=mib * 2**20)


def in_vmem(x):
    return pltpu.with_memory_space_constraint(x, pltpu.VMEM)


def in_hbm(x):
    return pltpu.with_memory_space_constraint(x, pltpu.HBM)


def two(x):
    high = x.astype(BF16)
    return high, (x - high.astype(F32)).astype(BF16)


def dot(a, b, dims=NN, precision=None):
    return lax.dot_general(a, b, dims, precision=precision, preferred_element_type=F32)


def correct_kernel(parts, place, grad, error, qt, high, low, pt, grads, errors, factors, total, sems, q_sem):
    rows, cols = high.shape
    rank = qt.shape[0]
    width = cols // parts
    take_q = pltpu.make_async_copy(qt, factors, q_sem)
    take_q.start()
    takes = []
    for part in range(parts):
        columns = pl.ds(part * width, width)
        takes.append(
            (
                pltpu.make_async_copy(error.at[0, :, columns], errors.at[:, columns], sems.at[0, part]),
                pltpu.make_async_copy(grad.at[0, :, columns], grads.at[:, columns], sems.at[1, part]),
            )
        )
        for take in takes[-1]:
            take.start()
    total[...] = jnp.zeros_like(total)
    take_q.wait()
    for part in range(parts):
        columns = pl.ds(part * width, width)
        for take in takes[part]:
            take.wait()
        hi, lo = two(grads[:, columns].astype(F32) + errors[:, columns])
        high[:, columns] = hi
        low[:, columns] = lo
        qh, ql = two(factors[:, columns])
        a = dot(jnp.concatenate([qh, ql], 0), hi, NT)
        total[...] += a[:rank] + a[rank:] + dot(qh, lo, NT)
    pt[...] = total[...]


def correct(place, grad, error, qt):
    _, rows, cols = grad.shape
    rank = qt.shape[0]
    parts = cols // 512
    return pl.pallas_call(
        functools.partial(correct_kernel, parts),
        in_specs=[pl.BlockSpec(memory_space=pltpu.SMEM)] + [pl.BlockSpec(memory_space=pltpu.HBM)] * 3,
        out_specs=[VMEM, VMEM, VMEM],
        out_shape=[
            pltpu.VMEM((rows, cols), BF16),
            pltpu.VMEM((rows, cols), BF16),
            pltpu.VMEM((rank, rows), F32),
        ],
        scratch_shapes=[
            pltpu.VMEM((rows, cols), BF16),
            pltpu.VMEM((rows, cols), F32),
            pltpu.VMEM((rank, cols), F32),
            pltpu.VMEM((rank, rows), F32),
            pltpu.SemaphoreType.DMA((2, parts)),
            pltpu.SemaphoreType.DMA,
        ],
        compiler_params=params(32),
        name="correct",
    )(place, in_hbm(grad), in_hbm(error), in_hbm(qt))


def terms_kernel(replicas, first, place, pt, high, low, terms, gram, mean):
    pieces, rank, width = terms.shape
    pm = pt[...] / replicas
    if gram is not None:
        mean[...] = pm
        gram[...] = jnp.zeros_like(gram)
        gram[:, :rank] = dot(pm, pm, NT, HIGHEST)
    ph, pl_ = two(pm)
    both = jnp.concatenate([ph, pl_], 0)
    here = place[0]

    def body(n, carry):
        columns = pl.ds(pl.multiple_of(((n + first) ^ here) * width, width), width)
        a = dot(both, high[:, columns])
        terms[n] = a[:rank] + a[rank:] + dot(ph, low[:, columns])
        return carry

    lax.fori_loop(0, pieces, body, 0, unroll=4)


def terms_of(place, pt, high, low, replicas, first, pieces, with_gram):
    rank, rows = pt.shape
    width = high.shape[1] // PIECES
    kernel = functools.partial(terms_kernel, replicas, first)
    shapes = [pltpu.VMEM((pieces, rank, width), F32)]
    if with_gram:
        shapes += [pltpu.VMEM((rank, GRAM_LANES), F32), pltpu.VMEM((rank, rows), F32)]
    return pl.pallas_call(
        kernel if with_gram else lambda *refs: kernel(*refs, None, None),
        in_specs=[pl.BlockSpec(memory_space=pltpu.SMEM), VMEM, VMEM, VMEM],
        out_specs=[VMEM] * len(shapes),
        out_shape=shapes,
        compiler_params=params(8),
        name="terms",
    )(place, pt, in_vmem(high), in_vmem(low))


def factor_kernel(gram, mean, inverse, left):
    rank = mean.shape[0]
    rows = mean.shape[1]
    i = lax.broadcasted_iota(jnp.int32, (rank, GRAM_LANES), 0)
    j = lax.broadcasted_iota(jnp.int32, (rank, GRAM_LANES), 1)
    total = gram[...]
    diagonal = jnp.where(i == j, total, 0.0)
    trace = jnp.sum(jnp.sum(diagonal, 1, keepdims=True), 0, keepdims=True)
    shift = 0.001 * trace / rank
    work = total + jnp.where(i == j, shift, 0.0) + jnp.where(j == i + rank, 1.0, 0.0)
    scale = jnp.zeros((rank, 1), F32)
    row_of = lax.broadcasted_iota(jnp.int32, (rank, 1), 0)
    for k in range(rank):
        pivot = work[k : k + 1, :]
        value = pivot[:, k : k + 1]
        scale = jnp.where(row_of == k, lax.rsqrt(value), scale)
        if k + 1 < rank:
            factor = jnp.where(row_of > k, work[:, k : k + 1] / value, 0.0)
            work = work - factor * pivot
    w = work[:, rank : 2 * rank] * scale
    inverse[...] = w
    hat = dot(w, mean[...], NN, HIGHEST).T
    h, l = two(hat)
    left[...] = jnp.concatenate([h, l, h, jnp.zeros((rows, 128 - 3 * rank), BF16)], 1)


def factor(gram, mean):
    rank, rows = mean.shape
    return pl.pallas_call(
        factor_kernel,
        in_specs=[VMEM, VMEM],
        out_specs=[VMEM, VMEM],
        out_shape=[pltpu.VMEM((rank, rank), F32), pltpu.VMEM((rows, 128), BF16)],
        compiler_params=params(8),
        name="factor",
    )(gram, mean)


def update_kernel(replicas, place, sums, inverse, left, high, low, new_error, update, qt, errors, updates, factors, right, sems):
    rank, width = sums.shape[1:]
    groups = errors.shape[0]
    each = sums.shape[0] // groups
    span = each * width
    group_here, piece_here = place[0] // each, place[0] % each
    right[3 * rank :, :] = jnp.zeros((128 - 3 * rank, right.shape[1]), BF16)
    for g in range(groups):
        for n in range(each):
            at = g * each + n
            q = dot(inverse[...], sums[at], NN, HIGHEST) / replicas
            factors[g, :, pl.ds(pl.multiple_of((n ^ piece_here) * width, width), width)] = q
            h, l = two(q)
            right[: 3 * rank, at * width : (at + 1) * width] = jnp.concatenate([h, h, l], 0)
    gives = []
    for g in range(groups):
        start = (g ^ group_here) * span
        for n in range(each):
            at = g * each + n
            inner = pl.multiple_of((n ^ piece_here) * width, width)
            columns = pl.ds(pl.multiple_of(start + inner, width), width)
            approx = dot(left[...], right[:, at * width : (at + 1) * width])
            updates[g, :, pl.ds(inner, width)] = approx.astype(BF16)
            errors[g, :, pl.ds(inner, width)] = (high[:, columns].astype(F32) - approx) + low[:, columns].astype(F32)
        columns = pl.ds(pl.multiple_of(start, span), span)
        for k, (source, target) in enumerate(
            ((errors.at[g], new_error.at[0, :, columns]), (updates.at[g], update.at[:, columns]), (factors.at[g], qt.at[:, columns]))
        ):
            gives.append(pltpu.make_async_copy(source, target, sems.at[k, g]))
            gives[-1].start()
    for give in gives:
        give.wait()


def update_of(place, sums, inverse, left, high, low, replicas):
    pieces, rank, width = sums.shape
    rows, cols = high.shape
    each = 4
    groups = pieces // each
    return pl.pallas_call(
        functools.partial(update_kernel, replicas),
        in_specs=[pl.BlockSpec(memory_space=pltpu.SMEM)] + [VMEM] * 5,
        out_specs=[pl.BlockSpec(memory_space=pltpu.HBM)] * 3,
        out_shape=[
            jax.ShapeDtypeStruct((1, rows, cols), F32),
            jax.ShapeDtypeStruct((rows, cols), BF16),
            jax.ShapeDtypeStruct((rank, cols), F32),
        ],
        scratch_shapes=[
            pltpu.VMEM((groups, rows, each * width), F32),
            pltpu.VMEM((groups, rows, each * width), BF16),
            pltpu.VMEM((groups, rank, each * width), F32),
            pltpu.VMEM((128, pieces * width), BF16),
            pltpu.SemaphoreType.DMA((3, groups)),
        ],
        compiler_params=params(32),
        name="update",
    )(place, sums, inverse, left, in_vmem(high), in_vmem(low))


def swap(x, mask):
    devices = lax.axis_size("rep") * lax.axis_size("fsdp")
    return lax.ppermute(x, AXES, [(i, i ^ mask) for i in range(devices)])


CORE, Y, X, Z_LOW, Z_HIGH = 8, 16, 1, 2, 4


def all_sum(kept, given, gram):
    rank, width = kept.shape[1:]
    gram = jnp.pad(gram, ((0, 0), (0, width - gram.shape[1])))[None]
    v = (kept + swap(given, CORE)).reshape(2, 2, 4, rank, width)
    over_x = swap(jnp.concatenate([v[0, 1], gram]), X)
    v = v[0, 0] + over_x[:4] + swap(v[1, 0], Y) + swap(v[1, 1], X ^ Y)
    gram = gram + over_x[4:]
    v = [jnp.concatenate([v[n : n + 1], gram]) for n in range(4)]
    v = (v[0] + swap(v[1], Z_LOW)) + (swap(v[2], Z_HIGH) + swap(v[3], Z_LOW ^ Z_HIGH))
    v, gram = v[0], v[1, :, :GRAM_LANES]
    v = jnp.stack([v, swap(v, Z_LOW), swap(v, Z_HIGH), swap(v, Z_LOW ^ Z_HIGH)])
    v = jnp.stack([v, swap(v, X), swap(v, Y), swap(v, X ^ Y)])
    v = jnp.stack([v, swap(v, CORE)])
    return v.reshape(PIECES, rank, width), gram


def local(grad, error, q_prev):
    replicas, shards = lax.axis_size("rep"), lax.axis_size("fsdp")
    paired = replicas == 4 and shards == 8
    if paired:
        r, f = lax.axis_index("rep"), lax.axis_index("fsdp")
        place = (r & 1) * 16 + (r >> 1) * 8 + (f & 1) * 4 + (f >> 1)
    else:
        place = 0
    place = jnp.asarray(place, jnp.int32).reshape(1)
    high, low, pt = correct(place, grad, error, q_prev.T)
    if paired:
        pt = pt + swap(pt, CORE)
        pt = pt + swap(pt, Y)
        half = PIECES // 2
        given, gram, mean = terms_of(place, pt, high, low, replicas, half, half, True)
        (kept,) = terms_of(place, pt, high, low, replicas, 0, half, False)
        sums, gram = all_sum(kept, given, gram)
    else:
        pt = lax.psum(pt, "rep")
        terms, gram, mean = terms_of(place, pt, high, low, replicas, 0, PIECES, True)
        sums, gram = lax.psum(terms, AXES), lax.psum(gram, "fsdp")
    inverse, left = factor(gram, mean)
    new_error, update, qt = update_of(place, sums, inverse, left, high, low, replicas)
    return update, new_error, qt.T


def solution(mesh):
    placed = (P("rep", "fsdp", None), P("rep", "fsdp", None), P())
    return jax.shard_map(
        local,
        mesh=mesh,
        in_specs=placed,
        out_specs=(P("fsdp", None), P("rep", "fsdp", None), P()),
        check_vma=False,
    )
```

time: 285 us -> 76.5 us (0.27)
  waiting for transfers between devices: 165 us -> 20.6 us
  matrix products: 63 us -> 0 us
  Pallas kernels: 0 us -> 32.7 us
  blocking collectives: 30.5 us -> 0 us
  starting transfers between devices: 0.08 us -> 21.6 us
  between operations: 14.7 us -> 0.94 us
  other arithmetic: 8.6 us -> 0.42 us
    psum x2 -> x0, waiting for transfers between devices: 165 us -> none  [the longest x1 133 us: local(): q_next = lax.psum(q_terms, ('rep', 'fsdp')) / replicas]
    dot_general x4 -> x0, matrix products: 61.9 us -> none  [the longest x1 23.3 us: local(): approx = jnp.dot(p_hat, q_next.T, precision=highest)]
    pallas_call x0 -> x5, Pallas kernels: none -> 32.7 us  [the longest x1 14.9 us: correct(): pl.pallas_call(functools.partial(correct_kernel, parts), in_specs=[pl.Blo...]
    psum x1 -> x0, blocking collectives: 30.5 us -> none  [local(): gram = lax.psum(jnp.dot(p_mean.T, p_mean, precision=highest), 'fsdp')]
    ppermute x0 -> x16, starting transfers between devices: none -> 21.6 us  [swap(): return lax.ppermute(x, AXES, [(i, i ^ mask) for i in range(devices)])]
    ppermute x0 -> x16, waiting for transfers between devices: none -> 20.6 us  [swap(): return lax.ppermute(x, AXES, [(i, i ^ mask) for i in range(devices)])]
    another operation x5 -> x3, other arithmetic: 6.68 us -> 0.23 us  [the longest x2 0.22 us: all_sum(): v = jnp.stack([v, swap(v, CORE)])]
  transfers between devices with their start and end apart: 2 -> 16, of which waited for: 2 -> 11; matrix products, arithmetic and copies ran while one was open for 0% -> 0% of each run, Pallas kernels for 0% -> 7%
where the time goes in v1:
time: 76.5 us; the launch traced here: 76.4 us
  Pallas kernels  32.7 us (43%)
  starting transfers between devices  21.6 us (28%)
  waiting for transfers between devices  20.6 us (27%)
  between operations  0.94 us (1%)
    ppermute x16, starting transfers between devices, swap(): return lax.ppermute(x, AXES, [(i, i ^ mask) for i in range(devices)])  21.6 us
    ppermute x16, waiting for transfers between devices, swap(): return lax.ppermute(x, AXES, [(i, i ^ mask) for i in range(devices)])  20.6 us
    pallas_call x1, Pallas kernels, correct(): pl.pallas_call(functools.partial(correct_kernel, parts), in_specs=[pl.Blo...  14.9 us
    pallas_call x1, Pallas kernels, update_of(): pl.pallas_call(functools.partial(update_kernel, replicas), in_specs=[pl.B...  10.4 us
    pallas_call x2, Pallas kernels, terms_of(): pl.pallas_call(kernel if with_gram else lambda *refs: kernel(*refs, None,...  4.08 us
    pallas_call x1, Pallas kernels, factor(): pl.pallas_call(factor_kernel, in_specs=[VMEM, VMEM], out_specs=[VMEM, VME...  3.31 us
  transfers between devices with their start and end apart: 16, of which 11 were waited for; matrix products, arithmetic and copies ran while one was open for 0% of the time, Pallas kernels for 7%

profile of v1, /device:TPU:1, one launch (start us, length us, event | category | flops | bytes accessed | tf_op | source)
XLA Modules:
  0.0 76.4 jit_solution(4879192828032837149)
XLA Ops:
  0.6 14.9 %correct.1 = (bf16[512,8192]{1,0:T(8,128)(2,1)S(1)}, bf16[512,8192]{1,0:T(8,128)(2,1)S(1)}, f32[32,512]{1,0:T(8,128)S(1)}) custom-call(s32[1]{0:T(128)} %bitcast.place.refs_0_, bf16[1,512,8192]{2,1,0:T(8,128)(2,1)} %grad.1, f32[1,512,8192]{2,1,0:T(8,128)} %error.1, f32[32,8192]{1,0:T(8,128)} %bitcast.37), custom_call_target="tpu_custom_call" | custom-call | tf_op jit(solution)/shard_map/correct/pallas_call | solution.py:77
  15.7 1.2 %collective-permute-done = f32[32,512]{1,0:T(8,128)S(1)} collective-permute-done((f32[32,512]{1,0:T(8,128)S(1)}, f32[32,512]{1,0:T(8,128)S(1)}, u32[]{:S(2)}, u32[]{:S(2)}) %collective-permute-start) | collective-permute-done | bytes 65568 | tf_op jit(solution)/shard_map/ppermute | solution.py:236
  16.9 2.5 %collective-permute-start.1 = (f32[32,512]{1,0:T(8,128)S(1)}, f32[32,512]{1,0:T(8,128)S(1)}, u32[]{:S(2)}, u32[]{:S(2)}) collective-permute-start(f32[32,512]{1,0:T(8,128)S(1)} %add.44), channel_id=1, source_target_pairs={{0,16},{1,17},{2,18},{3,19},{4,20},{5,21},{6,22},{7,23},{8,24},{9,... | collective-permute-start | bytes 196616 | tf_op jit(solution)/shard_map/ppermute | solution.py:236
  19.3 2.2 %collective-permute-done.1 = f32[32,512]{1,0:T(8,128)S(1)} collective-permute-done((f32[32,512]{1,0:T(8,128)S(1)}, f32[32,512]{1,0:T(8,128)S(1)}, u32[]{:S(2)}, u32[]{:S(2)}) %collective-permute-start.1) | collective-permute-done | bytes 65568 | tf_op jit(solution)/shard_map/ppermute | solution.py:236
  21.5 2.2 %terms.3 = (f32[16,32,256]{2,1,0:T(8,128)S(1)}, f32[32,128]{1,0:T(8,128)S(1)}, f32[32,512]{1,0:T(8,128)S(1)}) custom-call(s32[1]{0:T(128)} %bitcast.place.refs_0_, f32[32,512]{1,0:T(8,128)S(1)} %add.45.refs_1_.pt, bf16[512,8192]{1,0:T(8,128)(2,1)S(1)} %get-tuple-element.15.refs_2_.high, bf16[512,8192]{1,0:T(8,128)(2,1)S(1)} %get-tuple-element.16.refs_3_.low), custom_call_target="tpu_custom_call" | custom-call | tf_op jit(solution)/shard_map/terms/pallas_call | solution.py:126
  24.6 1.9 %terms.2 = f32[16,32,256]{2,1,0:T(8,128)S(1)} custom-call(s32[1]{0:T(128)} %bitcast.place.refs_0_, f32[32,512]{1,0:T(8,128)S(1)} %add.45.refs_1_.pt, bf16[512,8192]{1,0:T(8,128)(2,1)S(1)} %get-tuple-element.15.refs_2_.high, bf16[512,8192]{1,0:T(8,128)(2,1)S(1)} %get-tuple-element.16.refs_3_.low), custom_call_target="tpu_custom_call" | custom-call | tf_op jit(solution)/shard_map/terms/pallas_call | solution.py:126
  26.7 1.6 %collective-permute-start.3 = (f32[5,32,256]{2,1,0:T(8,128)S(1)}, f32[5,32,256]{2,1,0:T(8,128)S(1)}, u32[]{:S(2)}, u32[]{:S(2)}) collective-permute-start(f32[5,32,256]{2,1,0:T(8,128)S(1)} %pad_maximum_fusion.2), channel_id=1, source_target_pairs={{0,1},{1,0},{2,3},{3,2},{4,5},{5,4},{6,7},{7,6},{8,9},{9,8},{10,11... | collective-permute-start | bytes 491528 | tf_op jit(solution)/shard_map/ppermute | solution.py:236
  28.2 1.3 %collective-permute-start.4 = (f32[4,32,256]{2,1,0:T(8,128)S(1)}, f32[4,32,256]{2,1,0:T(8,128)S(1)}, u32[]{:S(2)}, u32[]{:S(2)}) collective-permute-start(f32[4,32,256]{2,1,0:T(8,128)S(1)} %get-tuple-element.27), channel_id=1, source_target_pairs={{0,16},{1,17},{2,18},{3,19},{4,20},{5,21},{6,22},{7,23},{8,24},{9,... | collective-permute-start | bytes 393224 | tf_op jit(solution)/shard_map/ppermute | solution.py:236
  29.5 3.5 %collective-permute-done.4 = f32[4,32,256]{2,1,0:T(8,128)S(1)} collective-permute-done((f32[4,32,256]{2,1,0:T(8,128)S(1)}, f32[4,32,256]{2,1,0:T(8,128)S(1)}, u32[]{:S(2)}, u32[]{:S(2)}) %collective-permute-start.4) | collective-permute-done | bytes 131104 | tf_op jit(solution)/shard_map/ppermute | solution.py:236
  33.0 3.6 %collective-permute-done.5 = f32[4,32,256]{2,1,0:T(8,128)S(1)} collective-permute-done((f32[4,32,256]{2,1,0:T(8,128)S(1)}, f32[4,32,256]{2,1,0:T(8,128)S(1)}, u32[]{:S(2)}, u32[]{:S(2)}) %collective-permute-start.5) | collective-permute-done | bytes 131104 | tf_op jit(solution)/shard_map/ppermute | solution.py:236
  36.7 3.4 %collective-permute-start.8 = (f32[2,32,256]{2,1,0:T(8,128)S(1)}, f32[2,32,256]{2,1,0:T(8,128)S(1)}, u32[]{:S(2)}, u32[]{:S(2)}) collective-permute-start(f32[2,32,256]{2,1,0:T(8,128)S(1)} %get-tuple-element.38), channel_id=1, source_target_pairs={{0,6},{1,7},{2,4},{3,5},{4,2},{5,3},{6,0},{7,1},{8,14},{9,15},{10,... | collective-permute-start | bytes 196616 | tf_op jit(solution)/shard_map/ppermute | solution.py:236
  40.4 1.3 %collective-permute-done.8 = f32[2,32,256]{2,1,0:T(8,128)S(1)} collective-permute-done((f32[2,32,256]{2,1,0:T(8,128)S(1)}, f32[2,32,256]{2,1,0:T(8,128)S(1)}, u32[]{:S(2)}, u32[]{:S(2)}) %collective-permute-start.8) | collective-permute-done | bytes 65568 | tf_op jit(solution)/shard_map/ppermute | solution.py:236
  41.8 3.3 %collective-permute-done.6 = f32[2,32,256]{2,1,0:T(8,128)S(1)} collective-permute-done((f32[2,32,256]{2,1,0:T(8,128)S(1)}, f32[2,32,256]{2,1,0:T(8,128)S(1)}, u32[]{:S(2)}, u32[]{:S(2)}) %collective-permute-start.6) | collective-permute-done | bytes 65568 | tf_op jit(solution)/shard_map/ppermute | solution.py:236
  45.1 1.2 %collective-permute-start.11 = (f32[32,256]{1,0:T(8,128)S(1)}, f32[32,256]{1,0:T(8,128)S(1)}, u32[]{:S(2)}, u32[]{:S(2)}) collective-permute-start(f32[32,256]{1,0:T(8,128)S(1)} %get-tuple-element.37), channel_id=1, source_target_pairs={{0,6},{1,7},{2,4},{3,5},{4,2},{5,3},{6,0},{7,1},{8,14},{9,15},{10,... | collective-permute-start | bytes 98312 | tf_op jit(solution)/shard_map/ppermute | solution.py:236
  46.9 1.8 %collective-permute-start.9 = (f32[32,256]{1,0:T(8,128)S(1)}, f32[32,256]{1,0:T(8,128)S(1)}, u32[]{:S(2)}, u32[]{:S(2)}) collective-permute-start(f32[32,256]{1,0:T(8,128)S(1)} %get-tuple-element.37), channel_id=1, source_target_pairs={{0,2},{1,3},{2,0},{3,1},{4,6},{5,7},{6,4},{7,5},{8,10},{9,11},{10,... | collective-permute-start | bytes 98312 | tf_op jit(solution)/shard_map/ppermute | solution.py:236
  48.7 1.0 %collective-permute-done.11 = f32[32,256]{1,0:T(8,128)S(1)} collective-permute-done((f32[32,256]{1,0:T(8,128)S(1)}, f32[32,256]{1,0:T(8,128)S(1)}, u32[]{:S(2)}, u32[]{:S(2)}) %collective-permute-start.11) | collective-permute-done | bytes 32800 | tf_op jit(solution)/shard_map/ppermute | solution.py:236
  50.5 2.3 %collective-permute-start.13 = (f32[4,32,256]{2,1,0:T(8,128)S(1)}, f32[4,32,256]{2,1,0:T(8,128)S(1)}, u32[]{:S(2)}, u32[]{:S(2)}) collective-permute-start(f32[4,32,256]{2,1,0:T(8,128)S(1)} %get-tuple-element.31), channel_id=1, source_target_pairs={{0,16},{1,17},{2,18},{3,19},{4,20},{5,21},{6,22},{7,23},{8,24},{9,... | collective-permute-start | bytes 393224 | tf_op jit(solution)/shard_map/ppermute | solution.py:236
  52.7 1.3 %collective-permute-start.14 = (f32[4,32,256]{2,1,0:T(8,128)S(1)}, f32[4,32,256]{2,1,0:T(8,128)S(1)}, u32[]{:S(2)}, u32[]{:S(2)}) collective-permute-start(f32[4,32,256]{2,1,0:T(8,128)S(1)} %get-tuple-element.31), channel_id=1, source_target_pairs={{0,17},{1,16},{2,19},{3,18},{4,21},{5,20},{6,23},{7,22},{8,25},{9,... | collective-permute-start | bytes 393224 | tf_op jit(solution)/shard_map/ppermute | solution.py:236
  54.0 1.1 %collective-permute-done.13 = f32[4,32,256]{2,1,0:T(8,128)S(1)} collective-permute-done((f32[4,32,256]{2,1,0:T(8,128)S(1)}, f32[4,32,256]{2,1,0:T(8,128)S(1)}, u32[]{:S(2)}, u32[]{:S(2)}) %collective-permute-start.13) | collective-permute-done | bytes 131104 | tf_op jit(solution)/shard_map/ppermute | solution.py:236
  55.1 1.5 %collective-permute-done.12 = f32[4,32,256]{2,1,0:T(8,128)S(1)} collective-permute-done((f32[4,32,256]{2,1,0:T(8,128)S(1)}, f32[4,32,256]{2,1,0:T(8,128)S(1)}, u32[]{:S(2)}, u32[]{:S(2)}) %collective-permute-start.12) | collective-permute-done | bytes 131104 | tf_op jit(solution)/shard_map/ppermute | solution.py:236
  56.5 1.3 %collective-permute-done.14 = f32[4,32,256]{2,1,0:T(8,128)S(1)} collective-permute-done((f32[4,32,256]{2,1,0:T(8,128)S(1)}, f32[4,32,256]{2,1,0:T(8,128)S(1)}, u32[]{:S(2)}, u32[]{:S(2)}) %collective-permute-start.14) | collective-permute-done | bytes 131104 | tf_op jit(solution)/shard_map/ppermute | solution.py:236
  57.9 4.4 %collective-permute-start.15 = (f32[4,4,32,256]{3,2,1,0:T(8,128)S(1)}, f32[4,4,32,256]{3,2,1,0:T(8,128)S(1)}, u32[]{:S(2)}, u32[]{:S(2)}) collective-permute-start(f32[4,4,32,256]{3,2,1,0:T(8,128)S(1)} %get-tuple-element.26), channel_id=1, source_target_pairs={{0,8},{1,9},{2,10},{3,11},{4,12},{5,13},{6,14},{7,15},{8,0},{9,1},... | collective-permute-start | bytes 1572872 | tf_op jit(solution)/shard_map/ppermute | solution.py:236
  62.3 3.3 %factor.1 = (f32[32,32]{1,0:T(8,128)S(1)}, bf16[512,128]{1,0:T(8,128)(2,1)S(1)}) custom-call(f32[32,128]{1,0:T(8,128)S(1)} %slice_bitcast_fusion.4.gram, f32[32,512]{1,0:T(8,128)S(1)} %get-tuple-element.19.mean), custom_call_target="tpu_custom_call" | custom-call | tf_op jit(solution)/shard_map/factor/pallas_call | solution.py:164
  65.8 10.4 %update.1 = (f32[1,512,8192]{2,1,0:T(8,128)}, bf16[512,8192]{1,0:T(8,128)(2,1)}, f32[32,8192]{1,0:T(8,128)}) custom-call(s32[1]{0:T(128)} %bitcast.place.refs_0_, f32[32,32,256]{2,1,0:T(8,128)S(1)} %bitcast.34, f32[32,32]{1,0:T(8,128)S(1)} %get-tuple-element.20.inverse, bf16[512,128]{1,0:T(8,128)(2,1)S(1)} %get-tuple-element.21.left, ...), custom_call_target="tpu_custom_call" | custom-call | tf_op jit(solution)/shard_map/update/pallas_call | solution.py:213
  (28 shorter events, 3.1 us)
Async XLA Ops:
  15.6 1.3 %collective-permute-start = (f32[32,512]{1,0:T(8,128)S(1)}, f32[32,512]{1,0:T(8,128)S(1)}, u32[]{:S(2)}, u32[]{:S(2)}) collective-permute-start(f32[32,512]{1,0:T(8,128)S(1)} %get-tuple-element.14), channel_id=1, source_target_pairs={{0,8},{1,9},{2,10},{3,11},{4,12},{5,13},{6,14},{7,15},{8,0},{9,1},... | collective-permute-start | bytes 196616 | tf_op jit(solution)/shard_map/ppermute | solution.py:236
  16.9 4.6 %collective-permute-start.1 = (f32[32,512]{1,0:T(8,128)S(1)}, f32[32,512]{1,0:T(8,128)S(1)}, u32[]{:S(2)}, u32[]{:S(2)}) collective-permute-start(f32[32,512]{1,0:T(8,128)S(1)} %add.44), channel_id=1, source_target_pairs={{0,16},{1,17},{2,18},{3,19},{4,20},{5,21},{6,22},{7,23},{8,24},{9,... | collective-permute-start | bytes 196616 | tf_op jit(solution)/shard_map/ppermute | solution.py:236
  23.8 2.8 %collective-permute-start.2 = (f32[16,32,256]{2,1,0:T(8,128)S(1)}, f32[16,32,256]{2,1,0:T(8,128)S(1)}, u32[]{:S(2)}, u32[]{:S(2)}) collective-permute-start(f32[16,32,256]{2,1,0:T(8,128)S(1)} %get-tuple-element.17), channel_id=1, source_target_pairs={{0,8},{1,9},{2,10},{3,11},{4,12},{5,13},{6,14},{7,15},{8,0},{9,1},... | collective-permute-start | bytes 1572872 | tf_op jit(solution)/shard_map/ppermute | solution.py:236
  26.7 9.9 %collective-permute-start.3 = (f32[5,32,256]{2,1,0:T(8,128)S(1)}, f32[5,32,256]{2,1,0:T(8,128)S(1)}, u32[]{:S(2)}, u32[]{:S(2)}) collective-permute-start(f32[5,32,256]{2,1,0:T(8,128)S(1)} %pad_maximum_fusion.2), channel_id=1, source_target_pairs={{0,1},{1,0},{2,3},{3,2},{4,5},{5,4},{6,7},{7,6},{8,9},{9,8},{10,11... | collective-permute-start | bytes 491528 | tf_op jit(solution)/shard_map/ppermute | solution.py:236
  28.2 4.8 %collective-permute-start.4 = (f32[4,32,256]{2,1,0:T(8,128)S(1)}, f32[4,32,256]{2,1,0:T(8,128)S(1)}, u32[]{:S(2)}, u32[]{:S(2)}) collective-permute-start(f32[4,32,256]{2,1,0:T(8,128)S(1)} %get-tuple-element.27), channel_id=1, source_target_pairs={{0,16},{1,17},{2,18},{3,19},{4,20},{5,21},{6,22},{7,23},{8,24},{9,... | collective-permute-start | bytes 393224 | tf_op jit(solution)/shard_map/ppermute | solution.py:236
  29.5 7.1 %collective-permute-start.5 = (f32[4,32,256]{2,1,0:T(8,128)S(1)}, f32[4,32,256]{2,1,0:T(8,128)S(1)}, u32[]{:S(2)}, u32[]{:S(2)}) collective-permute-start(f32[4,32,256]{2,1,0:T(8,128)S(1)} %get-tuple-element.28), channel_id=1, source_target_pairs={{0,17},{1,16},{2,19},{3,18},{4,21},{5,20},{6,23},{7,22},{8,25},{9,... | collective-permute-start | bytes 393224 | tf_op jit(solution)/shard_map/ppermute | solution.py:236
  36.7 5.1 %collective-permute-start.8 = (f32[2,32,256]{2,1,0:T(8,128)S(1)}, f32[2,32,256]{2,1,0:T(8,128)S(1)}, u32[]{:S(2)}, u32[]{:S(2)}) collective-permute-start(f32[2,32,256]{2,1,0:T(8,128)S(1)} %get-tuple-element.38), channel_id=1, source_target_pairs={{0,6},{1,7},{2,4},{3,5},{4,2},{5,3},{6,0},{7,1},{8,14},{9,15},{10,... | collective-permute-start | bytes 196616 | tf_op jit(solution)/shard_map/ppermute | solution.py:236
  40.1 5.0 %collective-permute-start.6 = (f32[2,32,256]{2,1,0:T(8,128)S(1)}, f32[2,32,256]{2,1,0:T(8,128)S(1)}, u32[]{:S(2)}, u32[]{:S(2)}) collective-permute-start(f32[2,32,256]{2,1,0:T(8,128)S(1)} %get-tuple-element.39), channel_id=1, source_target_pairs={{0,2},{1,3},{2,0},{3,1},{4,6},{5,7},{6,4},{7,5},{8,10},{9,11},{10,... | collective-permute-start | bytes 196616 | tf_op jit(solution)/shard_map/ppermute | solution.py:236
  40.1 5.0 %collective-permute-start.7 = (f32[2,32,256]{2,1,0:T(8,128)S(1)}, f32[2,32,256]{2,1,0:T(8,128)S(1)}, u32[]{:S(2)}, u32[]{:S(2)}) collective-permute-start(f32[2,32,256]{2,1,0:T(8,128)S(1)} %get-tuple-element.40), channel_id=1, source_target_pairs={{0,4},{1,5},{2,6},{3,7},{4,0},{5,1},{6,2},{7,3},{8,12},{9,13},{10,... | collective-permute-start | bytes 196616 | tf_op jit(solution)/shard_map/ppermute | solution.py:236
  45.1 4.6 %collective-permute-start.11 = (f32[32,256]{1,0:T(8,128)S(1)}, f32[32,256]{1,0:T(8,128)S(1)}, u32[]{:S(2)}, u32[]{:S(2)}) collective-permute-start(f32[32,256]{1,0:T(8,128)S(1)} %get-tuple-element.37), channel_id=1, source_target_pairs={{0,6},{1,7},{2,4},{3,5},{4,2},{5,3},{6,0},{7,1},{8,14},{9,15},{10,... | collective-permute-start | bytes 98312 | tf_op jit(solution)/shard_map/ppermute | solution.py:236
  46.3 4.1 %collective-permute-start.10 = (f32[32,256]{1,0:T(8,128)S(1)}, f32[32,256]{1,0:T(8,128)S(1)}, u32[]{:S(2)}, u32[]{:S(2)}) collective-permute-start(f32[32,256]{1,0:T(8,128)S(1)} %get-tuple-element.37), channel_id=1, source_target_pairs={{0,4},{1,5},{2,6},{3,7},{4,0},{5,1},{6,2},{7,3},{8,12},{9,13},{10,... | collective-permute-start | bytes 98312 | tf_op jit(solution)/shard_map/ppermute | solution.py:236
  46.9 3.5 %collective-permute-start.9 = (f32[32,256]{1,0:T(8,128)S(1)}, f32[32,256]{1,0:T(8,128)S(1)}, u32[]{:S(2)}, u32[]{:S(2)}) collective-permute-start(f32[32,256]{1,0:T(8,128)S(1)} %get-tuple-element.37), channel_id=1, source_target_pairs={{0,2},{1,3},{2,0},{3,1},{4,6},{5,7},{6,4},{7,5},{8,10},{9,11},{10,... | collective-permute-start | bytes 98312 | tf_op jit(solution)/shard_map/ppermute | solution.py:236
  50.5 4.6 %collective-permute-start.13 = (f32[4,32,256]{2,1,0:T(8,128)S(1)}, f32[4,32,256]{2,1,0:T(8,128)S(1)}, u32[]{:S(2)}, u32[]{:S(2)}) collective-permute-start(f32[4,32,256]{2,1,0:T(8,128)S(1)} %get-tuple-element.31), channel_id=1, source_target_pairs={{0,16},{1,17},{2,18},{3,19},{4,20},{5,21},{6,22},{7,23},{8,24},{9,... | collective-permute-start | bytes 393224 | tf_op jit(solution)/shard_map/ppermute | solution.py:236
  52.7 3.8 %collective-permute-start.12 = (f32[4,32,256]{2,1,0:T(8,128)S(1)}, f32[4,32,256]{2,1,0:T(8,128)S(1)}, u32[]{:S(2)}, u32[]{:S(2)}) collective-permute-start(f32[4,32,256]{2,1,0:T(8,128)S(1)} %get-tuple-element.31), channel_id=1, source_target_pairs={{0,1},{1,0},{2,3},{3,2},{4,5},{5,4},{6,7},{7,6},{8,9},{9,8},{10,11... | collective-permute-start | bytes 393224 | tf_op jit(solution)/shard_map/ppermute | solution.py:236
  52.7 5.1 %collective-permute-start.14 = (f32[4,32,256]{2,1,0:T(8,128)S(1)}, f32[4,32,256]{2,1,0:T(8,128)S(1)}, u32[]{:S(2)}, u32[]{:S(2)}) collective-permute-start(f32[4,32,256]{2,1,0:T(8,128)S(1)} %get-tuple-element.31), channel_id=1, source_target_pairs={{0,17},{1,16},{2,19},{3,18},{4,21},{5,20},{6,23},{7,22},{8,25},{9,... | collective-permute-start | bytes 393224 | tf_op jit(solution)/shard_map/ppermute | solution.py:236
  57.9 7.7 %collective-permute-start.15 = (f32[4,4,32,256]{3,2,1,0:T(8,128)S(1)}, f32[4,4,32,256]{3,2,1,0:T(8,128)S(1)}, u32[]{:S(2)}, u32[]{:S(2)}) collective-permute-start(f32[4,4,32,256]{3,2,1,0:T(8,128)S(1)} %get-tuple-element.26), channel_id=1, source_target_pairs={{0,8},{1,9},{2,10},{3,11},{4,12},{5,13},{6,14},{7,15},{8,0},{9,1},... | collective-permute-start | bytes 1572872 | tf_op jit(solution)/shard_map/ppermute | solution.py:236

commit v2 on v0

v2 whole, which is shorter than its diff:
```python
import functools

import jax
import jax.numpy as jnp
from jax import lax
from jax.experimental import pallas as pl
from jax.experimental.pallas import tpu as pltpu
from jax.sharding import PartitionSpec as P

F32, BF16 = jnp.float32, jnp.bfloat16
HIGHEST = lax.Precision.HIGHEST
AXES = ("rep", "fsdp")
NT = (((1,), (1,)), ((), ()))
NN = (((1,), (0,)), ((), ()))
VMEM = pl.BlockSpec(memory_space=pltpu.VMEM)
PIECES = 32
GROUP = PIECES // 8
GRAM_ROWS = 8


def params(mib):
    return pltpu.CompilerParams(vmem_limit_bytes=mib * 2**20)


def cost(microseconds):
    return pl.CostEstimate(flops=int(1e9 * microseconds), bytes_accessed=int(3.5e6 * microseconds), transcendentals=0)


def in_vmem(x):
    return pltpu.with_memory_space_constraint(x, pltpu.VMEM)


def in_hbm(x):
    return pltpu.with_memory_space_constraint(x, pltpu.HBM)


def two(x):
    high = x.astype(BF16)
    return high, (x - high.astype(F32)).astype(BF16)


def dot(a, b, dims=NN, precision=None):
    return lax.dot_general(a, b, dims, precision=precision, preferred_element_type=F32)


def correct_kernel(parts, grad, error, qt, high, low, pt, grads, errors, factors, total, sems):
    rows, cols = high.shape
    rank = qt.shape[0]
    width = cols // parts
    takes = []
    for part in range(parts):
        columns = pl.ds(part * width, width)
        takes.append(
            (
                pltpu.make_async_copy(error.at[0, :, columns], errors.at[:, columns], sems.at[0, part]),
                pltpu.make_async_copy(grad.at[0, :, columns], grads.at[:, columns], sems.at[1, part]),
                pltpu.make_async_copy(qt.at[:, columns], factors.at[:, columns], sems.at[2, part]),
            )
        )
        for take in takes[-1]:
            take.start()
    total[...] = jnp.zeros_like(total)
    for part in range(parts):
        columns = pl.ds(part * width, width)
        for take in takes[part]:
            take.wait()
        hi, lo = two(grads[:, columns].astype(F32) + errors[:, columns])
        high[:, columns] = hi
        low[:, columns] = lo
        qh, ql = two(factors[:, columns])
        a = dot(jnp.concatenate([qh, ql], 0), hi, NT)
        total[...] += a[:rank] + a[rank:] + dot(qh, lo, NT)
    pt[...] = total[...]


def correct(grad, error, qt):
    _, rows, cols = grad.shape
    rank = qt.shape[0]
    parts = cols // 512
    return pl.pallas_call(
        functools.partial(correct_kernel, parts),
        in_specs=[pl.BlockSpec(memory_space=pltpu.HBM)] * 3,
        out_specs=[VMEM, VMEM, VMEM],
        out_shape=[
            pltpu.VMEM((rows, cols), BF16),
            pltpu.VMEM((rows, cols), BF16),
            pltpu.VMEM((rank, rows), F32),
        ],
        scratch_shapes=[
            pltpu.VMEM((rows, cols), BF16),
            pltpu.VMEM((rows, cols), F32),
            pltpu.VMEM((rank, cols), F32),
            pltpu.VMEM((rank, rows), F32),
            pltpu.SemaphoreType.DMA((3, parts)),
        ],
        compiler_params=params(32),
        name="correct",
    )(in_hbm(grad), in_hbm(error), in_hbm(qt))


def terms_kernel(replicas, first, paired, pt, high, low, earlier, terms, mean=None):
    rank = pt.shape[0]
    width = high.shape[1] // PIECES
    pm = pt[...] / replicas
    ph, pl_ = two(pm)
    both = jnp.concatenate([ph, pl_], 0)
    here = first_piece(paired)
    if mean is None:
        gram = jnp.zeros((GRAM_ROWS, 128), F32)
    else:
        mean[...] = pm
        g = dot(pm, pm, NT, HIGHEST)
        gram = jnp.concatenate([g[n : n + GRAM_ROWS] for n in range(0, rank, GRAM_ROWS)], 1)
    at = 0
    for n in range(terms.shape[0] // (GROUP * rank * (width // 128))):
        for m in range(GROUP):
            columns = pl.ds(pl.multiple_of(((first + n * GROUP + m) ^ here) * width, width), width)
            a = dot(both, high[:, columns])
            a = a[:rank] + a[rank:] + dot(ph, low[:, columns])
            for k in range(0, width, 128):
                terms[at : at + rank] = a[:, k : k + 128]
                at += rank
        terms[at : at + GRAM_ROWS] = gram
        at += GRAM_ROWS


def terms_of(paired, pt, high, low, replicas, first, pieces, earlier, last):
    rank, rows = pt.shape
    tall = pieces * rank * (high.shape[1] // PIECES // 128) + pieces // GROUP * GRAM_ROWS
    shapes = [pltpu.VMEM((tall, 128), F32)] + [pltpu.VMEM((rank, rows), F32)] * last
    return pl.pallas_call(
        functools.partial(terms_kernel, replicas, first, paired),
        in_specs=[VMEM] * 4,
        out_specs=[VMEM] * len(shapes),
        out_shape=shapes,
        compiler_params=params(2),
        cost_estimate=cost(0.1 * pieces),
        name="terms",
    )(pt, in_vmem(high), in_vmem(low), earlier)


def factor_kernel(paired, gram, other, mean, inverse, left):
    rank, rows = mean.shape
    i = lax.broadcasted_iota(jnp.int32, (rank, 2 * rank), 0)
    j = lax.broadcasted_iota(jnp.int32, (rank, 2 * rank), 1)
    gram = gram[...]
    if paired:
        gram = jnp.where((lax.axis_index("rep") & 1) == 0, gram, other[...]) / 2
    total = jnp.concatenate([gram[:, n * rank : (n + 1) * rank] for n in range(rank // GRAM_ROWS)], 0)
    total = jnp.concatenate([total, jnp.zeros_like(total)], 1)
    diagonal = jnp.where(i == j, total, 0.0)
    trace = jnp.sum(jnp.sum(diagonal, 1, keepdims=True), 0, keepdims=True)
    shift = 0.001 * trace / rank
    work = total + jnp.where(i == j, shift, 0.0) + jnp.where(j == i + rank, 1.0, 0.0)
    scale = jnp.zeros((rank, 2 * rank), F32)
    for first in range(0, rank, 8):
        spread = [jnp.broadcast_to(work[:, k : k + 1], work.shape) for k in range(first, first + 8)]
        for n in range(8):
            k = first + n
            column = spread[n]
            value = column[k : k + 1]
            scale = jnp.where(i == k, lax.rsqrt(value), scale)
            ratio = jnp.where(i > k, column / value, 0.0)
            work = work - ratio * work[k : k + 1]
            for m in range(n + 1, 8):
                spread[m] = spread[m] - ratio * spread[m][k : k + 1]
    w = (work * scale)[:, rank:]
    inverse[...] = w
    hat = dot(w, mean[...], NN, HIGHEST).T
    h, l = two(hat)
    left[...] = jnp.concatenate([h, l, h, jnp.zeros((rows, 128 - 3 * rank), BF16)], 1)


def factor(paired, gram, other, mean):
    rank, rows = mean.shape
    return pl.pallas_call(
        functools.partial(factor_kernel, paired),
        in_specs=[VMEM] * 3,
        out_specs=[VMEM, VMEM],
        out_shape=[pltpu.VMEM((rank, rank), F32), pltpu.VMEM((rows, 128), BF16)],
        compiler_params=params(2),
        cost_estimate=cost(1.5),
        name="factor",
    )(gram, other, mean)


def update_kernel(replicas, spots, arrays, paired, inverse, left, high, low, *refs):
    new_error, update, qt, zero, errors, updates, factors, sems = refs[-8:]
    zero[...] = jnp.zeros_like(zero)
    count = len(spots)
    rank = inverse.shape[0]
    width = high.shape[1] // PIECES
    tall = rank * (width // 128)
    here = first_piece(paired)
    groups = [ref.at[n : n + GROUP * tall] for ref in refs[:arrays] for n in range(0, ref.shape[0], GROUP * tall)]
    gives = []
    for g in range(count):
        for n in range(GROUP):
            at = g * GROUP + n
            columns = pl.ds(pl.multiple_of(((spots[g] * GROUP + n) ^ here) * width, width), width)
            sums = jnp.concatenate([groups[g][k : k + rank] for k in range(n * tall, (n + 1) * tall, rank)], 1)
            q = dot(inverse[...], sums, NN, HIGHEST) / replicas
            factors[at] = q
            h, l = two(q)
            right = jnp.concatenate([h, h, l, jnp.zeros((128 - 3 * rank, width), BF16)], 0)
            approx = dot(left[...], right)
            updates[at] = approx.astype(BF16)
            errors[at] = (high[:, columns].astype(F32) - approx) + low[:, columns].astype(F32)
            for k, (source, target) in enumerate(
                ((errors, new_error.at[0, :, columns]), (updates, update.at[:, columns]), (factors, qt.at[:, columns]))
            ):
                gives.append(pltpu.make_async_copy(source.at[at], target, sems.at[k, at]))
                gives[-1].start()
    for give in gives:
        give.wait()


def update_of(paired, groups, spots, inverse, left, high, low, replicas, outs):
    rank = inverse.shape[0]
    rows, cols = high.shape
    count = len(groups)
    width = cols // PIECES
    pieces = len(spots) * GROUP
    fixed = 4 + count
    return pl.pallas_call(
        functools.partial(update_kernel, replicas, tuple(spots), len(groups), paired),
        in_specs=[VMEM] * (4 + count) + [pl.BlockSpec(memory_space=pltpu.HBM)] * len(outs),
        out_specs=[pl.BlockSpec(memory_space=pltpu.HBM)] * 3 + [VMEM],
        out_shape=[
            jax.ShapeDtypeStruct((1, rows, cols), F32),
            jax.ShapeDtypeStruct((rows, cols), BF16),
            jax.ShapeDtypeStruct((rank, cols), F32),
            pltpu.VMEM((8, 128), F32),
        ],
        input_output_aliases={fixed + n: n for n in range(len(outs))},
        scratch_shapes=[
            pltpu.VMEM((pieces, rows, width), F32),
            pltpu.VMEM((pieces, rows, width), BF16),
            pltpu.VMEM((pieces, rank, width), F32),
            pltpu.SemaphoreType.DMA((3, pieces)),
        ],
        compiler_params=params(pieces + 2),
        cost_estimate=cost(1 + 0.3 * pieces),
        name="update",
    )(inverse, left, in_vmem(high), in_vmem(low), *map(in_vmem, groups), *outs)


def first_piece(paired):
    if not paired:
        return 0
    r, f = lax.axis_index("rep"), lax.axis_index("fsdp")
    return GROUP * ((r & 1) * 4 + (r >> 1) * 2 + (f & 1))


def swap(x, mask, mask_one=None):
    devices = lax.axis_size("rep") * lax.axis_size("fsdp")
    masks = (mask, mask if mask_one is None else mask_one)
    return lax.ppermute(x, AXES, [(i, i ^ masks[i // CORE & 1]) for i in range(devices)])


CORE, Y, X, Z_LOW, Z_HIGH = 8, 16, 1, 2, 4


def paired_step(grad, error, qt, replicas):
    high, low, pt = correct(grad, error, qt)
    pt = pt + swap(pt, CORE)
    pt = pt + swap(pt, Y)
    half = PIECES // 2
    (given,) = terms_of(True, pt, high, low, replicas, half, half, pt, False)
    kept, mean = terms_of(True, pt, high, low, replicas, GROUP, half - GROUP, given, True)
    own, _ = terms_of(True, pt, high, low, replicas, 0, GROUP, kept, True)
    given = jnp.split(swap(given, CORE), [own.shape[0]])
    sums = [own + given[0]] + jnp.split(kept + given[1], 3)
    from_x, from_y, from_xy = swap(sums[1], X), swap(sums[2], Y), swap(sums[3], X ^ Y)
    own = (from_xy + from_y) + (from_x + sums[0])
    own = own + swap(own, Z_LOW, Z_HIGH)
    own = own + swap(own, Z_HIGH, Z_LOW)
    tall = own.shape[0] - GRAM_ROWS
    other = swap(own, CORE)
    own, gram = own[:tall], own[tall:]
    from_x, from_y, from_xy = swap(own, X), swap(own, Y), swap(own, X ^ Y)
    inverse, left = factor(True, gram, other[tall:], mean)
    *outs, zero = update_of(True, (own, other[:tall]), (0, 4), inverse, left, high, low, replicas, ())
    rest = jnp.concatenate([from_x, from_y, from_xy])
    others = swap(rest + zero[:1], CORE)
    *outs, _ = update_of(True, (from_x, from_y, from_xy), (1, 2, 3), inverse, left, high, low, replicas, outs)
    *outs, _ = update_of(True, (others,), (5, 6, 7), inverse, left, high, low, replicas, outs)
    return outs


def plain_step(grad, error, qt, replicas):
    high, low, pt = correct(grad, error, qt)
    pt = lax.psum(pt, "rep")
    terms, mean = terms_of(False, pt, high, low, replicas, 0, PIECES, pt, True)
    groups = jnp.split(lax.psum(terms, AXES), PIECES // GROUP)
    tall = groups[0].shape[0] - GRAM_ROWS
    gram = groups[0][tall:] / replicas
    inverse, left = factor(False, gram, gram, mean)
    groups = [group[:tall] for group in groups]
    *outs, _ = update_of(False, groups, range(len(groups)), inverse, left, high, low, replicas, ())
    return outs


def local(grad, error, q_prev):
    replicas, shards = lax.axis_size("rep"), lax.axis_size("fsdp")
    step = paired_step if (replicas, shards) == (4, 8) else plain_step
    new_error, update, qt = step(grad, error, q_prev.T, replicas)
    return update, new_error, qt.T


def solution(mesh):
    placed = (P("rep", "fsdp", None), P("rep", "fsdp", None), P())
    return jax.shard_map(
        local,
        mesh=mesh,
        in_specs=placed,
        out_specs=(P("fsdp", None), P("rep", "fsdp", None), P()),
        check_vma=False,
    )
```

time: 285 us -> 63.9 us (0.22)
  waiting for transfers between devices: 165 us -> 17.7 us
  matrix products: 63 us -> 0 us
  blocking collectives: 30.5 us -> 0 us
  Pallas kernels: 0 us -> 28.3 us
  starting transfers between devices: 0.08 us -> 16.6 us
  between operations: 14.7 us -> 0.9 us
  other arithmetic: 8.6 us -> 0.2 us
    psum x2 -> x0, waiting for transfers between devices: 165 us -> none  [the longest x1 133 us: local(): q_next = lax.psum(q_terms, ('rep', 'fsdp')) / replicas]
    dot_general x4 -> x0, matrix products: 61.9 us -> none  [the longest x1 23.3 us: local(): approx = jnp.dot(p_hat, q_next.T, precision=highest)]
    psum x1 -> x0, blocking collectives: 30.5 us -> none  [local(): gram = lax.psum(jnp.dot(p_mean.T, p_mean, precision=highest), 'fsdp')]
    pallas_call x0 -> x8, Pallas kernels: none -> 28.3 us  [the longest x3 13.5 us: update_of(): pl.pallas_call(functools.partial(update_kernel, replicas, tuple(spots), l...]
    ppermute x0 -> x13, waiting for transfers between devices: none -> 17.7 us  [swap(): lax.ppermute(x, AXES, [(i, i ^ masks[i // CORE & 1]) for i in range(devic...]
    ppermute x0 -> x13, starting transfers between devices: none -> 16.6 us  [swap(): lax.ppermute(x, AXES, [(i, i ^ masks[i // CORE & 1]) for i in range(devic...]
    another operation x5 -> x0, other arithmetic: 6.68 us -> none  [the longest x3 3.59 us: local(): chol = jnp.linalg.cholesky(gram + shift * jnp.eye(rank, dtype=jnp.float32))]
  transfers between devices with their start and end apart: 2 -> 13, of which waited for: 2 -> 8; matrix products, arithmetic and copies ran while one was open for 0% -> 0% of each run, Pallas kernels for 0% -> 19%
where the time goes in v2:
time: 63.9 us; the launch traced here: 63.8 us
  Pallas kernels  28.3 us (44%)
  waiting for transfers between devices  17.7 us (28%)
  starting transfers between devices  16.6 us (26%)
  between operations  0.9 us (1%)
    ppermute x13, waiting for transfers between devices, swap(): lax.ppermute(x, AXES, [(i, i ^ masks[i // CORE & 1]) for i in range(devic...  17.7 us
    ppermute x13, starting transfers between devices, swap(): lax.ppermute(x, AXES, [(i, i ^ masks[i // CORE & 1]) for i in range(devic...  16.6 us
    pallas_call x3, Pallas kernels, update_of(): pl.pallas_call(functools.partial(update_kernel, replicas, tuple(spots), l...  13.5 us
    pallas_call x1, Pallas kernels, correct(): pl.pallas_call(functools.partial(correct_kernel, parts), in_specs=[pl.Blo...  9.49 us
    pallas_call x3, Pallas kernels, terms_of(): pl.pallas_call(functools.partial(terms_kernel, replicas, first, paired),...  3.81 us
    pallas_call x1, Pallas kernels, factor(): pl.pallas_call(functools.partial(factor_kernel, paired), in_specs=[VMEM]...  1.45 us
  transfers between devices with their start and end apart: 13, of which 8 were waited for; matrix products, arithmetic and copies ran while one was open for 0% of the time, Pallas kernels for 19%

profile of v2, /device:TPU:1, one launch (start us, length us, event | category | flops | bytes accessed | tf_op | source)
XLA Modules:
  0.0 63.8 jit_solution(16921888018877871070)
XLA Ops:
  0.6 9.5 %correct.1 = (bf16[512,8192]{1,0:T(8,128)(2,1)S(1)}, bf16[512,8192]{1,0:T(8,128)(2,1)S(1)}, f32[32,512]{1,0:T(8,128)S(1)}) custom-call(bf16[1,512,8192]{2,1,0:T(8,128)(2,1)} %grad.1, f32[1,512,8192]{2,1,0:T(8,128)} %error.1, f32[32,8192]{1,0:T(8,128)} %bitcast.5), custom_call_target="tpu_custom_call" | custom-call | tf_op jit(solution)/shard_map/correct/pallas_call | solution.py:80
  10.3 1.2 %collective-permute-done = f32[32,512]{1,0:T(8,128)S(1)} collective-permute-done((f32[32,512]{1,0:T(8,128)S(1)}, f32[32,512]{1,0:T(8,128)S(1)}, u32[]{:S(2)}, u32[]{:S(2)}) %collective-permute-start) | collective-permute-done | bytes 65568 | tf_op jit(solution)/shard_map/ppermute | solution.py:258
  11.5 2.5 %collective-permute-start.1 = (f32[32,512]{1,0:T(8,128)S(1)}, f32[32,512]{1,0:T(8,128)S(1)}, u32[]{:S(2)}, u32[]{:S(2)}) collective-permute-start(f32[32,512]{1,0:T(8,128)S(1)} %add.37), channel_id=1, source_target_pairs={{0,16},{1,17},{2,18},{3,19},{4,20},{5,21},{6,22},{7,23},{8,24},{9,... | collective-permute-start | bytes 196616 | tf_op jit(solution)/shard_map/ppermute | solution.py:258
  13.9 2.2 %collective-permute-done.1 = f32[32,512]{1,0:T(8,128)S(1)} collective-permute-done((f32[32,512]{1,0:T(8,128)S(1)}, f32[32,512]{1,0:T(8,128)S(1)}, u32[]{:S(2)}, u32[]{:S(2)}) %collective-permute-start.1) | collective-permute-done | bytes 65568 | tf_op jit(solution)/shard_map/ppermute | solution.py:258
  16.1 1.6 %terms.3.earlier = f32[1056,128]{1,0:T(8,128)S(1)} custom-call(f32[32,512]{1,0:T(8,128)S(1)} %add.38.pt.earlier, bf16[512,8192]{1,0:T(8,128)(2,1)S(1)} %get-tuple-element.22.high, bf16[512,8192]{1,0:T(8,128)(2,1)S(1)} %get-tuple-element.23.low, f32[32,512]{1,0:T(8,128)S(1)} %add.38.pt.earlier), custom_call_target="tpu_custom_call" | custom-call | flops 1600000000 | bytes 5600000 | tf_op jit(solution)/shard_map/terms/pallas_call | solution.py:131
  17.7 0.9 %collective-permute-start.2 = (f32[1056,128]{1,0:T(8,128)S(1)}, f32[1056,128]{1,0:T(8,128)S(1)}, u32[]{:S(2)}, u32[]{:S(2)}) collective-permute-start(f32[1056,128]{1,0:T(8,128)S(1)} %terms.3.earlier), channel_id=1, source_target_pairs={{0,8},{1,9},{2,10},{3,11},{4,12},{5,13},{6,14},{7,15},{8,0},{9,1},... | collective-permute-start | bytes 1622024 | tf_op jit(solution)/shard_map/ppermute | solution.py:258
  18.5 1.2 %terms.4 = (f32[792,128]{1,0:T(8,128)S(1)}, f32[32,512]{1,0:T(8,128)S(1)}) custom-call(f32[32,512]{1,0:T(8,128)S(1)} %add.38.pt.earlier, bf16[512,8192]{1,0:T(8,128)(2,1)S(1)} %get-tuple-element.22.high, bf16[512,8192]{1,0:T(8,128)(2,1)S(1)} %get-tuple-element.23.low, f32[1056,128]{1,0:T(8,128)S(1)} %terms.3.earlier), custom_call_target="tpu_custom_call" | custom-call | flops 1200000000 | bytes 4200000 | tf_op jit(solution)/shard_map/terms/pallas_call | solution.py:131
  20.2 2.6 %collective-permute-start.3 = (f32[264,128]{1,0:T(8,128)S(1)}, f32[264,128]{1,0:T(8,128)S(1)}, u32[]{:S(2)}, u32[]{:S(2)}) collective-permute-start(f32[264,128]{1,0:T(8,128)S(1)} %get-tuple-element.41), channel_id=1, source_target_pairs={{0,17},{1,16},{2,19},{3,18},{4,21},{5,20},{6,23},{7,22},{8,25},{9,... | collective-permute-start | bytes 405512 | tf_op jit(solution)/shard_map/ppermute | solution.py:258
  23.1 1.0 %terms.5 = (f32[264,128]{1,0:T(8,128)S(1)}, f32[32,512]{1,0:T(8,128)}) custom-call(f32[32,512]{1,0:T(8,128)S(1)} %add.38.pt.earlier, bf16[512,8192]{1,0:T(8,128)(2,1)S(1)} %get-tuple-element.22.high, bf16[512,8192]{1,0:T(8,128)(2,1)S(1)} %get-tuple-element.23.low, f32[792,128]{1,0:T(8,128)S(1)} %get-tuple-element.24.earlier), custom_call_target="tpu_custom_call" | custom-call | flops 400000000 | bytes 1400000 | tf_op jit(solution)/shard_map/terms/pallas_call | solution.py:131
  24.2 2.1 %collective-permute-done.3 = f32[264,128]{1,0:T(8,128)S(1)} collective-permute-done((f32[264,128]{1,0:T(8,128)S(1)}, f32[264,128]{1,0:T(8,128)S(1)}, u32[]{:S(2)}, u32[]{:S(2)}) %collective-permute-start.3) | collective-permute-done | bytes 135200 | tf_op jit(solution)/shard_map/ppermute | solution.py:258
  26.3 3.5 %collective-permute-done.4 = f32[264,128]{1,0:T(8,128)S(1)} collective-permute-done((f32[264,128]{1,0:T(8,128)S(1)}, f32[264,128]{1,0:T(8,128)S(1)}, u32[]{:S(2)}, u32[]{:S(2)}) %collective-permute-start.4) | collective-permute-done | bytes 135200 | tf_op jit(solution)/shard_map/ppermute | solution.py:258
  29.8 2.6 %collective-permute-start.6 = (f32[264,128]{1,0:T(8,128)S(1)}, f32[264,128]{1,0:T(8,128)S(1)}, u32[]{:S(2)}, u32[]{:S(2)}) collective-permute-start(f32[264,128]{1,0:T(8,128)S(1)} %fusion.1), channel_id=1, source_target_pairs={{0,2},{1,3},{2,0},{3,1},{4,6},{5,7},{6,4},{7,5},{8,12},{9,13},{10,... | collective-permute-start | bytes 405512 | tf_op jit(solution)/shard_map/ppermute | solution.py:258
  32.3 3.9 %collective-permute-done.6 = f32[264,128]{1,0:T(8,128)S(1)} collective-permute-done((f32[264,128]{1,0:T(8,128)S(1)}, f32[264,128]{1,0:T(8,128)S(1)}, u32[]{:S(2)}, u32[]{:S(2)}) %collective-permute-start.6) | collective-permute-done | bytes 135200 | tf_op jit(solution)/shard_map/ppermute | solution.py:258
  36.2 0.8 %collective-permute-start.7 = (f32[264,128]{1,0:T(8,128)S(1)}, f32[264,128]{1,0:T(8,128)S(1)}, u32[]{:S(2)}, u32[]{:S(2)}) collective-permute-start(f32[264,128]{1,0:T(8,128)S(1)} %add.44), channel_id=1, source_target_pairs={{0,4},{1,5},{2,6},{3,7},{4,0},{5,1},{6,2},{7,3},{8,10},{9,11},{10,... | collective-permute-start | bytes 405512 | tf_op jit(solution)/shard_map/ppermute | solution.py:258
  37.0 3.2 %collective-permute-done.7 = f32[264,128]{1,0:T(8,128)S(1)} collective-permute-done((f32[264,128]{1,0:T(8,128)S(1)}, f32[264,128]{1,0:T(8,128)S(1)}, u32[]{:S(2)}, u32[]{:S(2)}) %collective-permute-start.7) | collective-permute-done | bytes 135200 | tf_op jit(solution)/shard_map/ppermute | solution.py:258
  40.2 3.0 %collective-permute-start.8 = (f32[264,128]{1,0:T(8,128)S(1)}, f32[264,128]{1,0:T(8,128)S(1)}, u32[]{:S(2)}, u32[]{:S(2)}) collective-permute-start(f32[264,128]{1,0:T(8,128)S(1)} %add.45), channel_id=1, source_target_pairs={{0,8},{1,9},{2,10},{3,11},{4,12},{5,13},{6,14},{7,15},{8,0},{9,1},... | collective-permute-start | bytes 405512 | tf_op jit(solution)/shard_map/ppermute | solution.py:258
  43.2 1.6 %collective-permute-start.10 = (f32[256,128]{1,0:T(8,128)S(1)}, f32[256,128]{1,0:T(8,128)S(1)}, u32[]{:S(2)}, u32[]{:S(2)}) collective-permute-start(f32[256,128]{1,0:T(8,128)S(1)} %slice.22.refs_0_), channel_id=1, source_target_pairs={{0,16},{1,17},{2,18},{3,19},{4,20},{5,21},{6,22},{7,23},{8,24},{9,... | collective-permute-start | bytes 393224 | tf_op jit(solution)/shard_map/ppermute | solution.py:258
  44.8 0.8 %collective-permute-start.11 = (f32[256,128]{1,0:T(8,128)S(1)}, f32[256,128]{1,0:T(8,128)S(1)}, u32[]{:S(2)}, u32[]{:S(2)}) collective-permute-start(f32[256,128]{1,0:T(8,128)S(1)} %slice.22.refs_0_), channel_id=1, source_target_pairs={{0,17},{1,16},{2,19},{3,18},{4,21},{5,20},{6,23},{7,22},{8,25},{9,... | collective-permute-start | bytes 393224 | tf_op jit(solution)/shard_map/ppermute | solution.py:258
  46.0 1.4 %factor.1 = (f32[32,32]{1,0:T(8,128)S(1)}, bf16[512,128]{1,0:T(8,128)(2,1)S(1)}) custom-call(f32[8,128]{1,0:T(8,128)S(1)} %slice.20.gram, f32[8,128]{1,0:T(8,128)S(1)} %slice.21.other, f32[32,512]{1,0:T(8,128)S(1)} %get-tuple-element.26.mean), custom_call_target="tpu_custom_call" | custom-call | flops 1500000000 | bytes 5250000 | tf_op jit(solution)/shard_map/factor/pallas_call | solution.py:176
  47.5 3.4 %update.3 = (f32[1,512,8192]{2,1,0:T(8,128)}, bf16[512,8192]{1,0:T(8,128)(2,1)}, f32[32,8192]{1,0:T(8,128)}, f32[8,128]{1,0:T(8,128)S(1)}) custom-call(f32[32,32]{1,0:T(8,128)S(1)} %get-tuple-element.27.inverse, bf16[512,128]{1,0:T(8,128)(2,1)S(1)} %get-tuple-element.28.left, bf16[512,8192]{1,0:T(8,128)(2,1)S(1)} %get-tuple-element.22.high, ...), custom_call_target="tpu_custom_call" | custom-call | flops 3400000000 | bytes 11900000 | tf_op jit(solution)/shard_map/update/pallas_call | solution.py:225
  50.9 1.4 %collective-permute-done.9.refs_0_ = f32[256,128]{1,0:T(8,128)S(1)} collective-permute-done((f32[256,128]{1,0:T(8,128)S(1)}, f32[256,128]{1,0:T(8,128)S(1)}, u32[]{:S(2)}, u32[]{:S(2)}) %collective-permute-start.9) | collective-permute-done | bytes 131104 | tf_op jit(solution)/shard_map/ppermute | solution.py:258
  52.4 1.0 %collective-permute-start.12 = (f32[768,128]{1,0:T(8,128)S(1)}, f32[768,128]{1,0:T(8,128)S(1)}, u32[]{:S(2)}, u32[]{:S(2)}) collective-permute-start(f32[768,128]{1,0:T(8,128)S(1)} %maximum_add_fusion), channel_id=1, source_target_pairs={{0,8},{1,9},{2,10},{3,11},{4,12},{5,13},{6,14},{7,15},{8,0},{9,1},... | collective-permute-start | bytes 1179656 | tf_op jit(solution)/shard_map/ppermute | solution.py:258
  53.4 5.1 %update.4 = (f32[1,512,8192]{2,1,0:T(8,128)}, bf16[512,8192]{1,0:T(8,128)(2,1)}, f32[32,8192]{1,0:T(8,128)}, f32[8,128]{1,0:T(8,128)}) custom-call(f32[32,32]{1,0:T(8,128)S(1)} %get-tuple-element.27.inverse, bf16[512,128]{1,0:T(8,128)(2,1)S(1)} %get-tuple-element.28.left, ...), custom_call_target="tpu_custom_call", output_to_operand_aliasing={{0}: (7, {}), {1}: (8, {}), {2}: (9, {})} | custom-call | flops 4600000000 | bytes 16099999 | tf_op jit(solution)/shard_map/update/pallas_call | solution.py:225
  58.5 5.1 %update.5 = (f32[1,512,8192]{2,1,0:T(8,128)}, bf16[512,8192]{1,0:T(8,128)(2,1)}, f32[32,8192]{1,0:T(8,128)}, f32[8,128]{1,0:T(8,128)}) custom-call(f32[32,32]{1,0:T(8,128)S(1)} %get-tuple-element.27.inverse, bf16[512,128]{1,0:T(8,128)(2,1)S(1)} %get-tuple-element.28.left, ...), custom_call_target="tpu_custom_call", output_to_operand_aliasing={{0}: (5, {}), {1}: (6, {}), {2}: (7, {})} | custom-call | flops 4600000000 | bytes 16099999 | tf_op jit(solution)/shard_map/update/pallas_call | solution.py:225
  (23 shorter events, 1.5 us)
Async XLA Ops:
  10.1 1.3 %collective-permute-start = (f32[32,512]{1,0:T(8,128)S(1)}, f32[32,512]{1,0:T(8,128)S(1)}, u32[]{:S(2)}, u32[]{:S(2)}) collective-permute-start(f32[32,512]{1,0:T(8,128)S(1)} %get-tuple-element.21), channel_id=1, source_target_pairs={{0,8},{1,9},{2,10},{3,11},{4,12},{5,13},{6,14},{7,15},{8,0},{9,1},... | collective-permute-start | bytes 196616 | tf_op jit(solution)/shard_map/ppermute | solution.py:258
  11.5 4.6 %collective-permute-start.1 = (f32[32,512]{1,0:T(8,128)S(1)}, f32[32,512]{1,0:T(8,128)S(1)}, u32[]{:S(2)}, u32[]{:S(2)}) collective-permute-start(f32[32,512]{1,0:T(8,128)S(1)} %add.37), channel_id=1, source_target_pairs={{0,16},{1,17},{2,18},{3,19},{4,20},{5,21},{6,22},{7,23},{8,24},{9,... | collective-permute-start | bytes 196616 | tf_op jit(solution)/shard_map/ppermute | solution.py:258
  17.7 2.4 %collective-permute-start.2 = (f32[1056,128]{1,0:T(8,128)S(1)}, f32[1056,128]{1,0:T(8,128)S(1)}, u32[]{:S(2)}, u32[]{:S(2)}) collective-permute-start(f32[1056,128]{1,0:T(8,128)S(1)} %terms.3.earlier), channel_id=1, source_target_pairs={{0,8},{1,9},{2,10},{3,11},{4,12},{5,13},{6,14},{7,15},{8,0},{9,1},... | collective-permute-start | bytes 1622024 | tf_op jit(solution)/shard_map/ppermute | solution.py:258
  20.2 6.1 %collective-permute-start.3 = (f32[264,128]{1,0:T(8,128)S(1)}, f32[264,128]{1,0:T(8,128)S(1)}, u32[]{:S(2)}, u32[]{:S(2)}) collective-permute-start(f32[264,128]{1,0:T(8,128)S(1)} %get-tuple-element.41), channel_id=1, source_target_pairs={{0,17},{1,16},{2,19},{3,18},{4,21},{5,20},{6,23},{7,22},{8,25},{9,... | collective-permute-start | bytes 405512 | tf_op jit(solution)/shard_map/ppermute | solution.py:258
  22.8 6.9 %collective-permute-start.4 = (f32[264,128]{1,0:T(8,128)S(1)}, f32[264,128]{1,0:T(8,128)S(1)}, u32[]{:S(2)}, u32[]{:S(2)}) collective-permute-start(f32[264,128]{1,0:T(8,128)S(1)} %get-tuple-element.39), channel_id=1, source_target_pairs={{0,16},{1,17},{2,18},{3,19},{4,20},{5,21},{6,22},{7,23},{8,24},{9,... | collective-permute-start | bytes 405512 | tf_op jit(solution)/shard_map/ppermute | solution.py:258
  23.0 6.7 %collective-permute-start.5 = (f32[264,128]{1,0:T(8,128)S(1)}, f32[264,128]{1,0:T(8,128)S(1)}, u32[]{:S(2)}, u32[]{:S(2)}) collective-permute-start(f32[264,128]{1,0:T(8,128)S(1)} %get-tuple-element.40), channel_id=1, source_target_pairs={{0,1},{1,0},{2,3},{3,2},{4,5},{5,4},{6,7},{7,6},{8,9},{9,8},{10,11... | collective-permute-start | bytes 405512 | tf_op jit(solution)/shard_map/ppermute | solution.py:258
  29.8 6.4 %collective-permute-start.6 = (f32[264,128]{1,0:T(8,128)S(1)}, f32[264,128]{1,0:T(8,128)S(1)}, u32[]{:S(2)}, u32[]{:S(2)}) collective-permute-start(f32[264,128]{1,0:T(8,128)S(1)} %fusion.1), channel_id=1, source_target_pairs={{0,2},{1,3},{2,0},{3,1},{4,6},{5,7},{6,4},{7,5},{8,12},{9,13},{10,... | collective-permute-start | bytes 405512 | tf_op jit(solution)/shard_map/ppermute | solution.py:258
  36.2 3.9 %collective-permute-start.7 = (f32[264,128]{1,0:T(8,128)S(1)}, f32[264,128]{1,0:T(8,128)S(1)}, u32[]{:S(2)}, u32[]{:S(2)}) collective-permute-start(f32[264,128]{1,0:T(8,128)S(1)} %add.44), channel_id=1, source_target_pairs={{0,4},{1,5},{2,6},{3,7},{4,0},{5,1},{6,2},{7,3},{8,10},{9,11},{10,... | collective-permute-start | bytes 405512 | tf_op jit(solution)/shard_map/ppermute | solution.py:258
  40.2 5.9 %collective-permute-start.8 = (f32[264,128]{1,0:T(8,128)S(1)}, f32[264,128]{1,0:T(8,128)S(1)}, u32[]{:S(2)}, u32[]{:S(2)}) collective-permute-start(f32[264,128]{1,0:T(8,128)S(1)} %add.45), channel_id=1, source_target_pairs={{0,8},{1,9},{2,10},{3,11},{4,12},{5,13},{6,14},{7,15},{8,0},{9,1},... | collective-permute-start | bytes 405512 | tf_op jit(solution)/shard_map/ppermute | solution.py:258
  43.2 7.8 %collective-permute-start.10 = (f32[256,128]{1,0:T(8,128)S(1)}, f32[256,128]{1,0:T(8,128)S(1)}, u32[]{:S(2)}, u32[]{:S(2)}) collective-permute-start(f32[256,128]{1,0:T(8,128)S(1)} %slice.22.refs_0_), channel_id=1, source_target_pairs={{0,16},{1,17},{2,18},{3,19},{4,20},{5,21},{6,22},{7,23},{8,24},{9,... | collective-permute-start | bytes 393224 | tf_op jit(solution)/shard_map/ppermute | solution.py:258
  44.8 6.2 %collective-permute-start.11 = (f32[256,128]{1,0:T(8,128)S(1)}, f32[256,128]{1,0:T(8,128)S(1)}, u32[]{:S(2)}, u32[]{:S(2)}) collective-permute-start(f32[256,128]{1,0:T(8,128)S(1)} %slice.22.refs_0_), channel_id=1, source_target_pairs={{0,17},{1,16},{2,19},{3,18},{4,21},{5,20},{6,23},{7,22},{8,25},{9,... | collective-permute-start | bytes 393224 | tf_op jit(solution)/shard_map/ppermute | solution.py:258
  45.6 6.8 %collective-permute-start.9 = (f32[256,128]{1,0:T(8,128)S(1)}, f32[256,128]{1,0:T(8,128)S(1)}, u32[]{:S(2)}, u32[]{:S(2)}) collective-permute-start(f32[256,128]{1,0:T(8,128)S(1)} %slice.22.refs_0_), channel_id=1, source_target_pairs={{0,1},{1,0},{2,3},{3,2},{4,5},{5,4},{6,7},{7,6},{8,9},{9,8},{10,11... | collective-permute-start | bytes 393224 | tf_op jit(solution)/shard_map/ppermute | solution.py:258
  52.4 6.1 %collective-permute-start.12 = (f32[768,128]{1,0:T(8,128)S(1)}, f32[768,128]{1,0:T(8,128)S(1)}, u32[]{:S(2)}, u32[]{:S(2)}) collective-permute-start(f32[768,128]{1,0:T(8,128)S(1)} %maximum_add_fusion), channel_id=1, source_target_pairs={{0,8},{1,9},{2,10},{3,11},{4,12},{5,13},{6,14},{7,15},{8,0},{9,1},... | collective-permute-start | bytes 1179656 | tf_op jit(solution)/shard_map/ppermute | solution.py:258

commit v3 on v2

--- a/solution.py
+++ b/solution.py
@@ -98,17 +98,17 @@
     )(in_hbm(grad), in_hbm(error), in_hbm(qt))
 
 
-def terms_kernel(replicas, first, paired, pt, high, low, earlier, terms, mean=None):
+def terms_kernel(replicas, first, paired, with_gram, pt, high, low, earlier, terms, *mean):
     rank = pt.shape[0]
     width = high.shape[1] // PIECES
     pm = pt[...] / replicas
     ph, pl_ = two(pm)
     both = jnp.concatenate([ph, pl_], 0)
     here = first_piece(paired)
-    if mean is None:
-        gram = jnp.zeros((GRAM_ROWS, 128), F32)
-    else:
-        mean[...] = pm
+    if mean:
+        mean[0][...] = pm
+    gram = jnp.zeros((GRAM_ROWS, 128), F32)
+    if with_gram:
         g = dot(pm, pm, NT, HIGHEST)
         gram = jnp.concatenate([g[n : n + GRAM_ROWS] for n in range(0, rank, GRAM_ROWS)], 1)
     at = 0
@@ -124,12 +124,12 @@
         at += GRAM_ROWS
 
 
-def terms_of(paired, pt, high, low, replicas, first, pieces, earlier, last):
+def terms_of(paired, pt, high, low, replicas, first, pieces, earlier, with_gram=False, with_mean=False):
     rank, rows = pt.shape
     tall = pieces * rank * (high.shape[1] // PIECES // 128) + pieces // GROUP * GRAM_ROWS
-    shapes = [pltpu.VMEM((tall, 128), F32)] + [pltpu.VMEM((rank, rows), F32)] * last
+    shapes = [pltpu.VMEM((tall, 128), F32)] + [pltpu.VMEM((rank, rows), F32)] * with_mean
     return pl.pallas_call(
-        functools.partial(terms_kernel, replicas, first, paired),
+        functools.partial(terms_kernel, replicas, first, paired, with_gram),
         in_specs=[VMEM] * 4,
         out_specs=[VMEM] * len(shapes),
         out_shape=shapes,
@@ -184,9 +184,10 @@
     )(gram, other, mean)
 
 
-def update_kernel(replicas, spots, arrays, paired, inverse, left, high, low, *refs):
-    new_error, update, qt, zero, errors, updates, factors, sems = refs[-8:]
-    zero[...] = jnp.zeros_like(zero)
+def update_kernel(replicas, spots, arrays, paired, with_zero, inverse, left, high, low, *refs):
+    new_error, update, qt, *zero, errors, updates, factors, sems = refs[-7 - with_zero :]
+    if with_zero:
+        zero[0][...] = jnp.zeros_like(zero[0])
     count = len(spots)
     rank = inverse.shape[0]
     width = high.shape[1] // PIECES
@@ -215,7 +216,7 @@
         give.wait()
 
 
-def update_of(paired, groups, spots, inverse, left, high, low, replicas, outs):
+def update_of(paired, groups, spots, inverse, left, high, low, replicas, outs, with_zero=False):
     rank = inverse.shape[0]
     rows, cols = high.shape
     count = len(groups)
@@ -223,15 +224,15 @@
     pieces = len(spots) * GROUP
     fixed = 4 + count
     return pl.pallas_call(
-        functools.partial(update_kernel, replicas, tuple(spots), len(groups), paired),
+        functools.partial(update_kernel, replicas, tuple(spots), len(groups), paired, with_zero),
         in_specs=[VMEM] * (4 + count) + [pl.BlockSpec(memory_space=pltpu.HBM)] * len(outs),
-        out_specs=[pl.BlockSpec(memory_space=pltpu.HBM)] * 3 + [VMEM],
+        out_specs=[pl.BlockSpec(memory_space=pltpu.HBM)] * 3 + [VMEM] * with_zero,
         out_shape=[
             jax.ShapeDtypeStruct((1, rows, cols), F32),
             jax.ShapeDtypeStruct((rows, cols), BF16),
             jax.ShapeDtypeStruct((rank, cols), F32),
-            pltpu.VMEM((8, 128), F32),
-        ],
+        ]
+        + [pltpu.VMEM((8, 128), F32)] * with_zero,
         input_output_aliases={fixed + n: n for n in range(len(outs))},
         scratch_shapes=[
             pltpu.VMEM((pieces, rows, width), F32),
@@ -266,9 +267,9 @@
     pt = pt + swap(pt, CORE)
     pt = pt + swap(pt, Y)
     half = PIECES // 2
-    (given,) = terms_of(True, pt, high, low, replicas, half, half, pt, False)
-    kept, mean = terms_of(True, pt, high, low, replicas, GROUP, half - GROUP, given, True)
-    own, _ = terms_of(True, pt, high, low, replicas, 0, GROUP, kept, True)
+    (given,) = terms_of(True, pt, high, low, replicas, half, half, pt)
+    kept, mean = terms_of(True, pt, high, low, replicas, GROUP, half - GROUP, given, True, True)
+    (own,) = terms_of(True, pt, high, low, replicas, 0, GROUP, kept, True)
     given = jnp.split(swap(given, CORE), [own.shape[0]])
     sums = [own + given[0]] + jnp.split(kept + given[1], 3)
     from_x, from_y, from_xy = swap(sums[1], X), swap(sums[2], Y), swap(sums[3], X ^ Y)
@@ -280,24 +281,24 @@
     own, gram = own[:tall], own[tall:]
     from_x, from_y, from_xy = swap(own, X), swap(own, Y), swap(own, X ^ Y)
     inverse, left = factor(True, gram, other[tall:], mean)
-    *outs, zero = update_of(True, (own, other[:tall]), (0, 4), inverse, left, high, low, replicas, ())
+    *outs, zero = update_of(True, (own, other[:tall]), (0, 4), inverse, left, high, low, replicas, (), True)
     rest = jnp.concatenate([from_x, from_y, from_xy])
     others = swap(rest + zero[:1], CORE)
-    *outs, _ = update_of(True, (from_x, from_y, from_xy), (1, 2, 3), inverse, left, high, low, replicas, outs)
-    *outs, _ = update_of(True, (others,), (5, 6, 7), inverse, left, high, low, replicas, outs)
+    outs = update_of(True, (from_x, from_y, from_xy), (1, 2, 3), inverse, left, high, low, replicas, outs)
+    outs = update_of(True, (others,), (5, 6, 7), inverse, left, high, low, replicas, outs)
     return outs
 
 
 def plain_step(grad, error, qt, replicas):
     high, low, pt = correct(grad, error, qt)
     pt = lax.psum(pt, "rep")
-    terms, mean = terms_of(False, pt, high, low, replicas, 0, PIECES, pt, True)
+    terms, mean = terms_of(False, pt, high, low, replicas, 0, PIECES, pt, True, True)
     groups = jnp.split(lax.psum(terms, AXES), PIECES // GROUP)
     tall = groups[0].shape[0] - GRAM_ROWS
     gram = groups[0][tall:] / replicas
     inverse, left = factor(False, gram, gram, mean)
     groups = [group[:tall] for group in groups]
-    *outs, _ = update_of(False, groups, range(len(groups)), inverse, left, high, low, replicas, ())
+    outs = update_of(False, groups, range(len(groups)), inverse, left, high, low, replicas, ())
     return outs
 
 

time: 63.9 us -> 62.7 us (0.981)
  Pallas kernels: 28.3 us -> 26.6 us
    pallas_call x3, Pallas kernels: 13.5 us -> 12.4 us  [update_of(): pl.pallas_call(functools.partial(update_kernel, replicas, tuple(spots), l...]
  transfers between devices with their start and end apart: 13 -> 13, of which waited for: 8 -> 8; matrix products, arithmetic and copies ran while one was open for 0% -> 0% of each run, Pallas kernels for 19% -> 18%
where the time goes in v3:
time: 62.7 us; the launch traced here: 62.6 us
  Pallas kernels  26.6 us (42%)
  waiting for transfers between devices  18.2 us (29%)
  starting transfers between devices  16.6 us (26%)
  between operations  0.91 us (1%)
    ppermute x13, waiting for transfers between devices, swap(): lax.ppermute(x, AXES, [(i, i ^ masks[i // CORE & 1]) for i in range(devic...  18.2 us
    ppermute x13, starting transfers between devices, swap(): lax.ppermute(x, AXES, [(i, i ^ masks[i // CORE & 1]) for i in range(devic...  16.6 us
    pallas_call x3, Pallas kernels, update_of(): pl.pallas_call(functools.partial(update_kernel, replicas, tuple(spots), l...  12.4 us
    pallas_call x1, Pallas kernels, correct(): pl.pallas_call(functools.partial(correct_kernel, parts), in_specs=[pl.Blo...  9.49 us
    pallas_call x3, Pallas kernels, terms_of(): pl.pallas_call(functools.partial(terms_kernel, replicas, first, paired, w...  3.3 us
    pallas_call x1, Pallas kernels, factor(): pl.pallas_call(functools.partial(factor_kernel, paired), in_specs=[VMEM]...  1.45 us
  transfers between devices with their start and end apart: 13, of which 8 were waited for; matrix products, arithmetic and copies ran while one was open for 0% of the time, Pallas kernels for 18%

profile of v3, /device:TPU:1, one launch (start us, length us, event | category | flops | bytes accessed | tf_op | source)
XLA Modules:
  0.0 62.6 jit_solution(17633018626431076664)
XLA Ops:
  0.6 9.5 %correct.1 = (bf16[512,8192]{1,0:T(8,128)(2,1)S(1)}, bf16[512,8192]{1,0:T(8,128)(2,1)S(1)}, f32[32,512]{1,0:T(8,128)S(1)}) custom-call(bf16[1,512,8192]{2,1,0:T(8,128)(2,1)} %grad.1, f32[1,512,8192]{2,1,0:T(8,128)} %error.1, f32[32,8192]{1,0:T(8,128)} %bitcast.5), custom_call_target="tpu_custom_call" | custom-call | tf_op jit(solution)/shard_map/correct/pallas_call | solution.py:80
  10.3 1.2 %collective-permute-done = f32[32,512]{1,0:T(8,128)S(1)} collective-permute-done((f32[32,512]{1,0:T(8,128)S(1)}, f32[32,512]{1,0:T(8,128)S(1)}, u32[]{:S(2)}, u32[]{:S(2)}) %collective-permute-start) | collective-permute-done | bytes 65568 | tf_op jit(solution)/shard_map/ppermute | solution.py:259
  11.5 2.5 %collective-permute-start.1 = (f32[32,512]{1,0:T(8,128)S(1)}, f32[32,512]{1,0:T(8,128)S(1)}, u32[]{:S(2)}, u32[]{:S(2)}) collective-permute-start(f32[32,512]{1,0:T(8,128)S(1)} %add.37), channel_id=1, source_target_pairs={{0,16},{1,17},{2,18},{3,19},{4,20},{5,21},{6,22},{7,23},{8,24},{9,... | collective-permute-start | bytes 196616 | tf_op jit(solution)/shard_map/ppermute | solution.py:259
  13.9 2.2 %collective-permute-done.1 = f32[32,512]{1,0:T(8,128)S(1)} collective-permute-done((f32[32,512]{1,0:T(8,128)S(1)}, f32[32,512]{1,0:T(8,128)S(1)}, u32[]{:S(2)}, u32[]{:S(2)}) %collective-permute-start.1) | collective-permute-done | bytes 65568 | tf_op jit(solution)/shard_map/ppermute | solution.py:259
  16.1 1.6 %terms.3.earlier = f32[1056,128]{1,0:T(8,128)S(1)} custom-call(f32[32,512]{1,0:T(8,128)S(1)} %add.38.pt.earlier, bf16[512,8192]{1,0:T(8,128)(2,1)S(1)} %get-tuple-element.21.high, bf16[512,8192]{1,0:T(8,128)(2,1)S(1)} %get-tuple-element.22.low, f32[32,512]{1,0:T(8,128)S(1)} %add.38.pt.earlier), custom_call_target="tpu_custom_call" | custom-call | flops 1600000000 | bytes 5600000 | tf_op jit(solution)/shard_map/terms/pallas_call | solution.py:131
  17.7 0.9 %collective-permute-start.2 = (f32[1056,128]{1,0:T(8,128)S(1)}, f32[1056,128]{1,0:T(8,128)S(1)}, u32[]{:S(2)}, u32[]{:S(2)}) collective-permute-start(f32[1056,128]{1,0:T(8,128)S(1)} %terms.3.earlier), channel_id=1, source_target_pairs={{0,8},{1,9},{2,10},{3,11},{4,12},{5,13},{6,14},{7,15},{8,0},{9,1},... | collective-permute-start | bytes 1622024 | tf_op jit(solution)/shard_map/ppermute | solution.py:259
  18.5 1.2 %terms.4 = (f32[792,128]{1,0:T(8,128)S(1)}, f32[32,512]{1,0:T(8,128)S(1)}) custom-call(f32[32,512]{1,0:T(8,128)S(1)} %add.38.pt.earlier, bf16[512,8192]{1,0:T(8,128)(2,1)S(1)} %get-tuple-element.21.high, bf16[512,8192]{1,0:T(8,128)(2,1)S(1)} %get-tuple-element.22.low, f32[1056,128]{1,0:T(8,128)S(1)} %terms.3.earlier), custom_call_target="tpu_custom_call" | custom-call | flops 1200000000 | bytes 4200000 | tf_op jit(solution)/shard_map/terms/pallas_call | solution.py:131
  20.2 2.6 %collective-permute-start.3 = (f32[264,128]{1,0:T(8,128)S(1)}, f32[264,128]{1,0:T(8,128)S(1)}, u32[]{:S(2)}, u32[]{:S(2)}) collective-permute-start(f32[264,128]{1,0:T(8,128)S(1)} %get-tuple-element.39), channel_id=1, source_target_pairs={{0,17},{1,16},{2,19},{3,18},{4,21},{5,20},{6,23},{7,22},{8,25},{9,... | collective-permute-start | bytes 405512 | tf_op jit(solution)/shard_map/ppermute | solution.py:259
  23.1 0.5 terms.5
  23.6 2.6 %collective-permute-done.3 = f32[264,128]{1,0:T(8,128)S(1)} collective-permute-done((f32[264,128]{1,0:T(8,128)S(1)}, f32[264,128]{1,0:T(8,128)S(1)}, u32[]{:S(2)}, u32[]{:S(2)}) %collective-permute-start.3) | collective-permute-done | bytes 135200 | tf_op jit(solution)/shard_map/ppermute | solution.py:259
  26.2 3.5 %collective-permute-done.4 = f32[264,128]{1,0:T(8,128)S(1)} collective-permute-done((f32[264,128]{1,0:T(8,128)S(1)}, f32[264,128]{1,0:T(8,128)S(1)}, u32[]{:S(2)}, u32[]{:S(2)}) %collective-permute-start.4) | collective-permute-done | bytes 135200 | tf_op jit(solution)/shard_map/ppermute | solution.py:259
  29.7 2.6 %collective-permute-start.6 = (f32[264,128]{1,0:T(8,128)S(1)}, f32[264,128]{1,0:T(8,128)S(1)}, u32[]{:S(2)}, u32[]{:S(2)}) collective-permute-start(f32[264,128]{1,0:T(8,128)S(1)} %fusion.1), channel_id=1, source_target_pairs={{0,2},{1,3},{2,0},{3,1},{4,6},{5,7},{6,4},{7,5},{8,12},{9,13},{10,... | collective-permute-start | bytes 405512 | tf_op jit(solution)/shard_map/ppermute | solution.py:259
  32.3 3.9 %collective-permute-done.6 = f32[264,128]{1,0:T(8,128)S(1)} collective-permute-done((f32[264,128]{1,0:T(8,128)S(1)}, f32[264,128]{1,0:T(8,128)S(1)}, u32[]{:S(2)}, u32[]{:S(2)}) %collective-permute-start.6) | collective-permute-done | bytes 135200 | tf_op jit(solution)/shard_map/ppermute | solution.py:259
  36.2 0.8 %collective-permute-start.7 = (f32[264,128]{1,0:T(8,128)S(1)}, f32[264,128]{1,0:T(8,128)S(1)}, u32[]{:S(2)}, u32[]{:S(2)}) collective-permute-start(f32[264,128]{1,0:T(8,128)S(1)} %add.44), channel_id=1, source_target_pairs={{0,4},{1,5},{2,6},{3,7},{4,0},{5,1},{6,2},{7,3},{8,10},{9,11},{10,... | collective-permute-start | bytes 405512 | tf_op jit(solution)/shard_map/ppermute | solution.py:259
  36.9 3.2 %collective-permute-done.7 = f32[264,128]{1,0:T(8,128)S(1)} collective-permute-done((f32[264,128]{1,0:T(8,128)S(1)}, f32[264,128]{1,0:T(8,128)S(1)}, u32[]{:S(2)}, u32[]{:S(2)}) %collective-permute-start.7) | collective-permute-done | bytes 135200 | tf_op jit(solution)/shard_map/ppermute | solution.py:259
  40.1 3.0 %collective-permute-start.8 = (f32[264,128]{1,0:T(8,128)S(1)}, f32[264,128]{1,0:T(8,128)S(1)}, u32[]{:S(2)}, u32[]{:S(2)}) collective-permute-start(f32[264,128]{1,0:T(8,128)S(1)} %add.45), channel_id=1, source_target_pairs={{0,8},{1,9},{2,10},{3,11},{4,12},{5,13},{6,14},{7,15},{8,0},{9,1},... | collective-permute-start | bytes 405512 | tf_op jit(solution)/shard_map/ppermute | solution.py:259
  43.1 1.6 %collective-permute-start.10 = (f32[256,128]{1,0:T(8,128)S(1)}, f32[256,128]{1,0:T(8,128)S(1)}, u32[]{:S(2)}, u32[]{:S(2)}) collective-permute-start(f32[256,128]{1,0:T(8,128)S(1)} %slice.22.refs_0_), channel_id=1, source_target_pairs={{0,16},{1,17},{2,18},{3,19},{4,20},{5,21},{6,22},{7,23},{8,24},{9,... | collective-permute-start | bytes 393224 | tf_op jit(solution)/shard_map/ppermute | solution.py:259
  44.7 0.8 %collective-permute-start.11 = (f32[256,128]{1,0:T(8,128)S(1)}, f32[256,128]{1,0:T(8,128)S(1)}, u32[]{:S(2)}, u32[]{:S(2)}) collective-permute-start(f32[256,128]{1,0:T(8,128)S(1)} %slice.22.refs_0_), channel_id=1, source_target_pairs={{0,17},{1,16},{2,19},{3,18},{4,21},{5,20},{6,23},{7,22},{8,25},{9,... | collective-permute-start | bytes 393224 | tf_op jit(solution)/shard_map/ppermute | solution.py:259
  46.0 1.4 %factor.1 = (f32[32,32]{1,0:T(8,128)S(1)}, bf16[512,128]{1,0:T(8,128)(2,1)S(1)}) custom-call(f32[8,128]{1,0:T(8,128)S(1)} %slice.20.gram, f32[8,128]{1,0:T(8,128)S(1)} %slice.21.other, f32[32,512]{1,0:T(8,128)S(1)} %get-tuple-element.24.mean), custom_call_target="tpu_custom_call" | custom-call | flops 1500000000 | bytes 5250000 | tf_op jit(solution)/shard_map/factor/pallas_call | solution.py:176
  47.5 3.4 %update.3 = (f32[1,512,8192]{2,1,0:T(8,128)}, bf16[512,8192]{1,0:T(8,128)(2,1)}, f32[32,8192]{1,0:T(8,128)}, f32[8,128]{1,0:T(8,128)S(1)}) custom-call(f32[32,32]{1,0:T(8,128)S(1)} %get-tuple-element.25.inverse, bf16[512,128]{1,0:T(8,128)(2,1)S(1)} %get-tuple-element.26.left, bf16[512,8192]{1,0:T(8,128)(2,1)S(1)} %get-tuple-element.21.high, ...), custom_call_target="tpu_custom_call" | custom-call | flops 3400000000 | bytes 11900000 | tf_op jit(solution)/shard_map/update/pallas_call | solution.py:226
  50.9 1.4 %collective-permute-done.9.refs_0_ = f32[256,128]{1,0:T(8,128)S(1)} collective-permute-done((f32[256,128]{1,0:T(8,128)S(1)}, f32[256,128]{1,0:T(8,128)S(1)}, u32[]{:S(2)}, u32[]{:S(2)}) %collective-permute-start.9) | collective-permute-done | bytes 131104 | tf_op jit(solution)/shard_map/ppermute | solution.py:259
  52.4 1.0 %collective-permute-start.12 = (f32[768,128]{1,0:T(8,128)S(1)}, f32[768,128]{1,0:T(8,128)S(1)}, u32[]{:S(2)}, u32[]{:S(2)}) collective-permute-start(f32[768,128]{1,0:T(8,128)S(1)} %maximum_add_fusion), channel_id=1, source_target_pairs={{0,8},{1,9},{2,10},{3,11},{4,12},{5,13},{6,14},{7,15},{8,0},{9,1},... | collective-permute-start | bytes 1179656 | tf_op jit(solution)/shard_map/ppermute | solution.py:259
  53.4 4.5 %update.4 = (f32[1,512,8192]{2,1,0:T(8,128)}, bf16[512,8192]{1,0:T(8,128)(2,1)}, f32[32,8192]{1,0:T(8,128)}) custom-call(f32[32,32]{1,0:T(8,128)S(1)} %get-tuple-element.25.inverse, bf16[512,128]{1,0:T(8,128)(2,1)S(1)} %get-tuple-element.26.left, ...), custom_call_target="tpu_custom_call", output_to_operand_aliasing={{0}: (7, {}), {1}: (8, {}), {2}: (9, {})} | custom-call | flops 4600000000 | bytes 16099999 | tf_op jit(solution)/shard_map/update/pallas_call | solution.py:226
  57.9 4.5 %update.5 = (f32[1,512,8192]{2,1,0:T(8,128)}, bf16[512,8192]{1,0:T(8,128)(2,1)}, f32[32,8192]{1,0:T(8,128)}) custom-call(f32[32,32]{1,0:T(8,128)S(1)} %get-tuple-element.25.inverse, bf16[512,128]{1,0:T(8,128)(2,1)S(1)} %get-tuple-element.26.left, ...), custom_call_target="tpu_custom_call", output_to_operand_aliasing={{0}: (5, {}), {1}: (6, {}), {2}: (7, {})} | custom-call | flops 4600000000 | bytes 16099999 | tf_op jit(solution)/shard_map/update/pallas_call | solution.py:226
  (23 shorter events, 1.5 us)
Async XLA Ops:
  10.1 1.3 %collective-permute-start = (f32[32,512]{1,0:T(8,128)S(1)}, f32[32,512]{1,0:T(8,128)S(1)}, u32[]{:S(2)}, u32[]{:S(2)}) collective-permute-start(f32[32,512]{1,0:T(8,128)S(1)} %get-tuple-element.20), channel_id=1, source_target_pairs={{0,8},{1,9},{2,10},{3,11},{4,12},{5,13},{6,14},{7,15},{8,0},{9,1},... | collective-permute-start | bytes 196616 | tf_op jit(solution)/shard_map/ppermute | solution.py:259
  11.5 4.6 %collective-permute-start.1 = (f32[32,512]{1,0:T(8,128)S(1)}, f32[32,512]{1,0:T(8,128)S(1)}, u32[]{:S(2)}, u32[]{:S(2)}) collective-permute-start(f32[32,512]{1,0:T(8,128)S(1)} %add.37), channel_id=1, source_target_pairs={{0,16},{1,17},{2,18},{3,19},{4,20},{5,21},{6,22},{7,23},{8,24},{9,... | collective-permute-start | bytes 196616 | tf_op jit(solution)/shard_map/ppermute | solution.py:259
  17.7 2.4 %collective-permute-start.2 = (f32[1056,128]{1,0:T(8,128)S(1)}, f32[1056,128]{1,0:T(8,128)S(1)}, u32[]{:S(2)}, u32[]{:S(2)}) collective-permute-start(f32[1056,128]{1,0:T(8,128)S(1)} %terms.3.earlier), channel_id=1, source_target_pairs={{0,8},{1,9},{2,10},{3,11},{4,12},{5,13},{6,14},{7,15},{8,0},{9,1},... | collective-permute-start | bytes 1622024 | tf_op jit(solution)/shard_map/ppermute | solution.py:259
  20.2 6.1 %collective-permute-start.3 = (f32[264,128]{1,0:T(8,128)S(1)}, f32[264,128]{1,0:T(8,128)S(1)}, u32[]{:S(2)}, u32[]{:S(2)}) collective-permute-start(f32[264,128]{1,0:T(8,128)S(1)} %get-tuple-element.39), channel_id=1, source_target_pairs={{0,17},{1,16},{2,19},{3,18},{4,21},{5,20},{6,23},{7,22},{8,25},{9,... | collective-permute-start | bytes 405512 | tf_op jit(solution)/shard_map/ppermute | solution.py:259
  22.8 6.9 %collective-permute-start.4 = (f32[264,128]{1,0:T(8,128)S(1)}, f32[264,128]{1,0:T(8,128)S(1)}, u32[]{:S(2)}, u32[]{:S(2)}) collective-permute-start(f32[264,128]{1,0:T(8,128)S(1)} %get-tuple-element.37), channel_id=1, source_target_pairs={{0,16},{1,17},{2,18},{3,19},{4,20},{5,21},{6,22},{7,23},{8,24},{9,... | collective-permute-start | bytes 405512 | tf_op jit(solution)/shard_map/ppermute | solution.py:259
  23.0 6.7 %collective-permute-start.5 = (f32[264,128]{1,0:T(8,128)S(1)}, f32[264,128]{1,0:T(8,128)S(1)}, u32[]{:S(2)}, u32[]{:S(2)}) collective-permute-start(f32[264,128]{1,0:T(8,128)S(1)} %get-tuple-element.38), channel_id=1, source_target_pairs={{0,1},{1,0},{2,3},{3,2},{4,5},{5,4},{6,7},{7,6},{8,9},{9,8},{10,11... | collective-permute-start | bytes 405512 | tf_op jit(solution)/shard_map/ppermute | solution.py:259
  29.7 6.4 %collective-permute-start.6 = (f32[264,128]{1,0:T(8,128)S(1)}, f32[264,128]{1,0:T(8,128)S(1)}, u32[]{:S(2)}, u32[]{:S(2)}) collective-permute-start(f32[264,128]{1,0:T(8,128)S(1)} %fusion.1), channel_id=1, source_target_pairs={{0,2},{1,3},{2,0},{3,1},{4,6},{5,7},{6,4},{7,5},{8,12},{9,13},{10,... | collective-permute-start | bytes 405512 | tf_op jit(solution)/shard_map/ppermute | solution.py:259
  36.2 3.9 %collective-permute-start.7 = (f32[264,128]{1,0:T(8,128)S(1)}, f32[264,128]{1,0:T(8,128)S(1)}, u32[]{:S(2)}, u32[]{:S(2)}) collective-permute-start(f32[264,128]{1,0:T(8,128)S(1)} %add.44), channel_id=1, source_target_pairs={{0,4},{1,5},{2,6},{3,7},{4,0},{5,1},{6,2},{7,3},{8,10},{9,11},{10,... | collective-permute-start | bytes 405512 | tf_op jit(solution)/shard_map/ppermute | solution.py:259
  40.1 5.9 %collective-permute-start.8 = (f32[264,128]{1,0:T(8,128)S(1)}, f32[264,128]{1,0:T(8,128)S(1)}, u32[]{:S(2)}, u32[]{:S(2)}) collective-permute-start(f32[264,128]{1,0:T(8,128)S(1)} %add.45), channel_id=1, source_target_pairs={{0,8},{1,9},{2,10},{3,11},{4,12},{5,13},{6,14},{7,15},{8,0},{9,1},... | collective-permute-start | bytes 405512 | tf_op jit(solution)/shard_map/ppermute | solution.py:259
  43.1 7.8 %collective-permute-start.10 = (f32[256,128]{1,0:T(8,128)S(1)}, f32[256,128]{1,0:T(8,128)S(1)}, u32[]{:S(2)}, u32[]{:S(2)}) collective-permute-start(f32[256,128]{1,0:T(8,128)S(1)} %slice.22.refs_0_), channel_id=1, source_target_pairs={{0,16},{1,17},{2,18},{3,19},{4,20},{5,21},{6,22},{7,23},{8,24},{9,... | collective-permute-start | bytes 393224 | tf_op jit(solution)/shard_map/ppermute | solution.py:259
  44.7 6.2 %collective-permute-start.11 = (f32[256,128]{1,0:T(8,128)S(1)}, f32[256,128]{1,0:T(8,128)S(1)}, u32[]{:S(2)}, u32[]{:S(2)}) collective-permute-start(f32[256,128]{1,0:T(8,128)S(1)} %slice.22.refs_0_), channel_id=1, source_target_pairs={{0,17},{1,16},{2,19},{3,18},{4,21},{5,20},{6,23},{7,22},{8,25},{9,... | collective-permute-start | bytes 393224 | tf_op jit(solution)/shard_map/ppermute | solution.py:259
  45.6 6.8 %collective-permute-start.9 = (f32[256,128]{1,0:T(8,128)S(1)}, f32[256,128]{1,0:T(8,128)S(1)}, u32[]{:S(2)}, u32[]{:S(2)}) collective-permute-start(f32[256,128]{1,0:T(8,128)S(1)} %slice.22.refs_0_), channel_id=1, source_target_pairs={{0,1},{1,0},{2,3},{3,2},{4,5},{5,4},{6,7},{7,6},{8,9},{9,8},{10,11... | collective-permute-start | bytes 393224 | tf_op jit(solution)/shard_map/ppermute | solution.py:259
  52.4 5.5 %collective-permute-start.12 = (f32[768,128]{1,0:T(8,128)S(1)}, f32[768,128]{1,0:T(8,128)S(1)}, u32[]{:S(2)}, u32[]{:S(2)}) collective-permute-start(f32[768,128]{1,0:T(8,128)S(1)} %maximum_add_fusion), channel_id=1, source_target_pairs={{0,8},{1,9},{2,10},{3,11},{4,12},{5,13},{6,14},{7,15},{8,0},{9,1},... | collective-permute-start | bytes 1179656 | tf_op jit(solution)/shard_map/ppermute | solution.py:259

commit v4 on v3

--- a/solution.py
+++ b/solution.py
@@ -267,13 +267,13 @@
     pt = pt + swap(pt, CORE)
     pt = pt + swap(pt, Y)
     half = PIECES // 2
-    (given,) = terms_of(True, pt, high, low, replicas, half, half, pt)
+    (given,) = terms_of(True, pt, high, low, replicas, half + GROUP, half - GROUP, pt)
     kept, mean = terms_of(True, pt, high, low, replicas, GROUP, half - GROUP, given, True, True)
-    (own,) = terms_of(True, pt, high, low, replicas, 0, GROUP, kept, True)
-    given = jnp.split(swap(given, CORE), [own.shape[0]])
-    sums = [own + given[0]] + jnp.split(kept + given[1], 3)
-    from_x, from_y, from_xy = swap(sums[1], X), swap(sums[2], Y), swap(sums[3], X ^ Y)
-    own = (from_xy + from_y) + (from_x + sums[0])
+    at_x, at_y, at_xy = jnp.split(kept + swap(given, CORE), 3)
+    from_x, from_y, from_xy = swap(at_x, X), swap(at_y, Y), swap(at_xy, X ^ Y)
+    (late,) = terms_of(True, pt, high, low, replicas, half, GROUP, from_xy)
+    (own,) = terms_of(True, pt, high, low, replicas, 0, GROUP, late, True)
+    own = (from_xy + from_y) + (from_x + (own + swap(late, CORE)))
     own = own + swap(own, Z_LOW, Z_HIGH)
     own = own + swap(own, Z_HIGH, Z_LOW)
     tall = own.shape[0] - GRAM_ROWS

time: 62.7 us -> 62 us (0.989)
  waiting for transfers between devices: 18.2 us -> 16.3 us
  starting transfers between devices: 16.6 us -> 17.8 us
    ppermute x13 -> x14, waiting for transfers between devices: 18.2 us -> 16.3 us  [swap(): lax.ppermute(x, AXES, [(i, i ^ masks[i // CORE & 1]) for i in range(devic...]
    ppermute x13 -> x14, starting transfers between devices: 16.6 us -> 17.8 us  [swap(): lax.ppermute(x, AXES, [(i, i ^ masks[i // CORE & 1]) for i in range(devic...]
    pallas_call x3 -> x4, Pallas kernels: 3.3 us -> 3.41 us  [terms_of(): pl.pallas_call(functools.partial(terms_kernel, replicas, first, paired, w...]
  transfers between devices with their start and end apart: 13 -> 14, of which waited for: 8 -> 9; matrix products, arithmetic and copies ran while one was open for 0% -> 0% of each run, Pallas kernels for 18% -> 19%
where the time goes in v4:
time: 62 us; the launch traced here: 61.9 us
  Pallas kernels  26.7 us (43%)
  starting transfers between devices  17.8 us (29%)
  waiting for transfers between devices  16.3 us (26%)
  between operations  0.9 us (1%)
    ppermute x14, starting transfers between devices, swap(): lax.ppermute(x, AXES, [(i, i ^ masks[i // CORE & 1]) for i in range(devic...  17.8 us
    ppermute x14, waiting for transfers between devices, swap(): lax.ppermute(x, AXES, [(i, i ^ masks[i // CORE & 1]) for i in range(devic...  16.3 us
    pallas_call x3, Pallas kernels, update_of(): pl.pallas_call(functools.partial(update_kernel, replicas, tuple(spots), l...  12.4 us
    pallas_call x1, Pallas kernels, correct(): pl.pallas_call(functools.partial(correct_kernel, parts), in_specs=[pl.Blo...  9.49 us
    pallas_call x4, Pallas kernels, terms_of(): pl.pallas_call(functools.partial(terms_kernel, replicas, first, paired, w...  3.41 us
    pallas_call x1, Pallas kernels, factor(): pl.pallas_call(functools.partial(factor_kernel, paired), in_specs=[VMEM]...  1.45 us
  transfers between devices with their start and end apart: 14, of which 9 were waited for; matrix products, arithmetic and copies ran while one was open for 0% of the time, Pallas kernels for 19%

profile of v4, /device:TPU:1, one launch (start us, length us, event | category | flops | bytes accessed | tf_op | source)
XLA Modules:
  0.0 61.9 jit_solution(18375137826636645604)
XLA Ops:
  0.6 9.5 %correct.1 = (bf16[512,8192]{1,0:T(8,128)(2,1)S(1)}, bf16[512,8192]{1,0:T(8,128)(2,1)S(1)}, f32[32,512]{1,0:T(8,128)S(1)}) custom-call(bf16[1,512,8192]{2,1,0:T(8,128)(2,1)} %grad.1, f32[1,512,8192]{2,1,0:T(8,128)} %error.1, f32[32,8192]{1,0:T(8,128)} %bitcast.5), custom_call_target="tpu_custom_call" | custom-call | tf_op jit(solution)/shard_map/correct/pallas_call | solution.py:80
  10.3 1.2 %collective-permute-done = f32[32,512]{1,0:T(8,128)S(1)} collective-permute-done((f32[32,512]{1,0:T(8,128)S(1)}, f32[32,512]{1,0:T(8,128)S(1)}, u32[]{:S(2)}, u32[]{:S(2)}) %collective-permute-start) | collective-permute-done | bytes 65568 | tf_op jit(solution)/shard_map/ppermute | solution.py:259
  11.5 2.5 %collective-permute-start.1 = (f32[32,512]{1,0:T(8,128)S(1)}, f32[32,512]{1,0:T(8,128)S(1)}, u32[]{:S(2)}, u32[]{:S(2)}) collective-permute-start(f32[32,512]{1,0:T(8,128)S(1)} %add.37), channel_id=1, source_target_pairs={{0,16},{1,17},{2,18},{3,19},{4,20},{5,21},{6,22},{7,23},{8,24},{9,... | collective-permute-start | bytes 196616 | tf_op jit(solution)/shard_map/ppermute | solution.py:259
  13.9 2.2 %collective-permute-done.1 = f32[32,512]{1,0:T(8,128)S(1)} collective-permute-done((f32[32,512]{1,0:T(8,128)S(1)}, f32[32,512]{1,0:T(8,128)S(1)}, u32[]{:S(2)}, u32[]{:S(2)}) %collective-permute-start.1) | collective-permute-done | bytes 65568 | tf_op jit(solution)/shard_map/ppermute | solution.py:259
  16.1 1.2 %terms.4.earlier = f32[792,128]{1,0:T(8,128)S(1)} custom-call(f32[32,512]{1,0:T(8,128)S(1)} %add.38.pt.earlier, bf16[512,8192]{1,0:T(8,128)(2,1)S(1)} %get-tuple-element.21.high, bf16[512,8192]{1,0:T(8,128)(2,1)S(1)} %get-tuple-element.22.low, f32[32,512]{1,0:T(8,128)S(1)} %add.38.pt.earlier), custom_call_target="tpu_custom_call" | custom-call | flops 1200000000 | bytes 4200000 | tf_op jit(solution)/shard_map/terms/pallas_call | solution.py:131
  17.3 0.9 %collective-permute-start.2 = (f32[792,128]{1,0:T(8,128)S(1)}, f32[792,128]{1,0:T(8,128)S(1)}, u32[]{:S(2)}, u32[]{:S(2)}) collective-permute-start(f32[792,128]{1,0:T(8,128)S(1)} %terms.4.earlier), channel_id=1, source_target_pairs={{0,8},{1,9},{2,10},{3,11},{4,12},{5,13},{6,14},{7,15},{8,0},{9,1},... | collective-permute-start | bytes 1216520 | tf_op jit(solution)/shard_map/ppermute | solution.py:259
  18.2 1.2 %terms.5 = (f32[792,128]{1,0:T(8,128)S(1)}, f32[32,512]{1,0:T(8,128)S(1)}) custom-call(f32[32,512]{1,0:T(8,128)S(1)} %add.38.pt.earlier, bf16[512,8192]{1,0:T(8,128)(2,1)S(1)} %get-tuple-element.21.high, bf16[512,8192]{1,0:T(8,128)(2,1)S(1)} %get-tuple-element.22.low, f32[792,128]{1,0:T(8,128)S(1)} %terms.4.earlier), custom_call_target="tpu_custom_call" | custom-call | flops 1200000000 | bytes 4200000 | tf_op jit(solution)/shard_map/terms/pallas_call | solution.py:131
  19.7 2.6 %collective-permute-start.3 = (f32[264,128]{1,0:T(8,128)S(1)}, f32[264,128]{1,0:T(8,128)S(1)}, u32[]{:S(2)}, u32[]{:S(2)}) collective-permute-start(f32[264,128]{1,0:T(8,128)S(1)} %get-tuple-element.39), channel_id=1, source_target_pairs={{0,17},{1,16},{2,19},{3,18},{4,21},{5,20},{6,23},{7,22},{8,25},{9,... | collective-permute-start | bytes 405512 | tf_op jit(solution)/shard_map/ppermute | solution.py:259
  22.6 3.1 %collective-permute-done.3.earlier = f32[264,128]{1,0:T(8,128)S(1)} collective-permute-done((f32[264,128]{1,0:T(8,128)S(1)}, f32[264,128]{1,0:T(8,128)S(1)}, u32[]{:S(2)}, u32[]{:S(2)}) %collective-permute-start.3) | collective-permute-done | bytes 135200 | tf_op jit(solution)/shard_map/ppermute | solution.py:259
  26.2 1.2 %collective-permute-start.6 = (f32[264,128]{1,0:T(8,128)S(1)}, f32[264,128]{1,0:T(8,128)S(1)}, u32[]{:S(2)}, u32[]{:S(2)}) collective-permute-start(f32[264,128]{1,0:T(8,128)S(1)} %terms.6.earlier), channel_id=1, source_target_pairs={{0,8},{1,9},{2,10},{3,11},{4,12},{5,13},{6,14},{7,15},{8,0},{9,1},... | collective-permute-start | bytes 405512 | tf_op jit(solution)/shard_map/ppermute | solution.py:259
  27.9 1.2 %collective-permute-done.4 = f32[264,128]{1,0:T(8,128)S(1)} collective-permute-done((f32[264,128]{1,0:T(8,128)S(1)}, f32[264,128]{1,0:T(8,128)S(1)}, u32[]{:S(2)}, u32[]{:S(2)}) %collective-permute-start.4) | collective-permute-done | bytes 135200 | tf_op jit(solution)/shard_map/ppermute | solution.py:259
  29.2 2.6 %collective-permute-start.7 = (f32[264,128]{1,0:T(8,128)S(1)}, f32[264,128]{1,0:T(8,128)S(1)}, u32[]{:S(2)}, u32[]{:S(2)}) collective-permute-start(f32[264,128]{1,0:T(8,128)S(1)} %add_add_fusion), channel_id=1, source_target_pairs={{0,2},{1,3},{2,0},{3,1},{4,6},{5,7},{6,4},{7,5},{8,12},{9,13},{10,... | collective-permute-start | bytes 405512 | tf_op jit(solution)/shard_map/ppermute | solution.py:259
  31.8 3.9 %collective-permute-done.7 = f32[264,128]{1,0:T(8,128)S(1)} collective-permute-done((f32[264,128]{1,0:T(8,128)S(1)}, f32[264,128]{1,0:T(8,128)S(1)}, u32[]{:S(2)}, u32[]{:S(2)}) %collective-permute-start.7) | collective-permute-done | bytes 135200 | tf_op jit(solution)/shard_map/ppermute | solution.py:259
  35.6 0.8 %collective-permute-start.8 = (f32[264,128]{1,0:T(8,128)S(1)}, f32[264,128]{1,0:T(8,128)S(1)}, u32[]{:S(2)}, u32[]{:S(2)}) collective-permute-start(f32[264,128]{1,0:T(8,128)S(1)} %add.44), channel_id=1, source_target_pairs={{0,4},{1,5},{2,6},{3,7},{4,0},{5,1},{6,2},{7,3},{8,10},{9,11},{10,... | collective-permute-start | bytes 405512 | tf_op jit(solution)/shard_map/ppermute | solution.py:259
  36.4 3.2 %collective-permute-done.8 = f32[264,128]{1,0:T(8,128)S(1)} collective-permute-done((f32[264,128]{1,0:T(8,128)S(1)}, f32[264,128]{1,0:T(8,128)S(1)}, u32[]{:S(2)}, u32[]{:S(2)}) %collective-permute-start.8) | collective-permute-done | bytes 135200 | tf_op jit(solution)/shard_map/ppermute | solution.py:259
  39.6 3.0 %collective-permute-start.9 = (f32[264,128]{1,0:T(8,128)S(1)}, f32[264,128]{1,0:T(8,128)S(1)}, u32[]{:S(2)}, u32[]{:S(2)}) collective-permute-start(f32[264,128]{1,0:T(8,128)S(1)} %add.45), channel_id=1, source_target_pairs={{0,8},{1,9},{2,10},{3,11},{4,12},{5,13},{6,14},{7,15},{8,0},{9,1},... | collective-permute-start | bytes 405512 | tf_op jit(solution)/shard_map/ppermute | solution.py:259
  42.6 1.2 %collective-permute-start.10 = (f32[256,128]{1,0:T(8,128)S(1)}, f32[256,128]{1,0:T(8,128)S(1)}, u32[]{:S(2)}, u32[]{:S(2)}) collective-permute-start(f32[256,128]{1,0:T(8,128)S(1)} %slice.22.refs_0_), channel_id=1, source_target_pairs={{0,1},{1,0},{2,3},{3,2},{4,5},{5,4},{6,7},{7,6},{8,9},{9,8},{10,11... | collective-permute-start | bytes 393224 | tf_op jit(solution)/shard_map/ppermute | solution.py:259
  43.9 1.4 %collective-permute-start.11 = (f32[256,128]{1,0:T(8,128)S(1)}, f32[256,128]{1,0:T(8,128)S(1)}, u32[]{:S(2)}, u32[]{:S(2)}) collective-permute-start(f32[256,128]{1,0:T(8,128)S(1)} %slice.22.refs_0_), channel_id=1, source_target_pairs={{0,16},{1,17},{2,18},{3,19},{4,20},{5,21},{6,22},{7,23},{8,24},{9,... | collective-permute-start | bytes 393224 | tf_op jit(solution)/shard_map/ppermute | solution.py:259
  45.4 1.4 %factor.1 = (f32[32,32]{1,0:T(8,128)S(1)}, bf16[512,128]{1,0:T(8,128)(2,1)S(1)}) custom-call(f32[8,128]{1,0:T(8,128)S(1)} %slice.20.gram, f32[8,128]{1,0:T(8,128)S(1)} %slice.21.other, f32[32,512]{1,0:T(8,128)S(1)} %get-tuple-element.24.mean), custom_call_target="tpu_custom_call" | custom-call | flops 1500000000 | bytes 5250000 | tf_op jit(solution)/shard_map/factor/pallas_call | solution.py:176
  46.9 3.4 %update.3 = (f32[1,512,8192]{2,1,0:T(8,128)}, bf16[512,8192]{1,0:T(8,128)(2,1)}, f32[32,8192]{1,0:T(8,128)}, f32[8,128]{1,0:T(8,128)S(1)}) custom-call(f32[32,32]{1,0:T(8,128)S(1)} %get-tuple-element.25.inverse, bf16[512,128]{1,0:T(8,128)(2,1)S(1)} %get-tuple-element.26.left, bf16[512,8192]{1,0:T(8,128)(2,1)S(1)} %get-tuple-element.21.high, ...), custom_call_target="tpu_custom_call" | custom-call | flops 3400000000 | bytes 11900000 | tf_op jit(solution)/shard_map/update/pallas_call | solution.py:226
  50.5 1.1 %collective-permute-done.12.refs_2_ = f32[256,128]{1,0:T(8,128)S(1)} collective-permute-done((f32[256,128]{1,0:T(8,128)S(1)}, f32[256,128]{1,0:T(8,128)S(1)}, u32[]{:S(2)}, u32[]{:S(2)}) %collective-permute-start.12) | collective-permute-done | bytes 131104 | tf_op jit(solution)/shard_map/ppermute | solution.py:259
  51.7 1.0 %collective-permute-start.13 = (f32[768,128]{1,0:T(8,128)S(1)}, f32[768,128]{1,0:T(8,128)S(1)}, u32[]{:S(2)}, u32[]{:S(2)}) collective-permute-start(f32[768,128]{1,0:T(8,128)S(1)} %maximum_add_fusion), channel_id=1, source_target_pairs={{0,8},{1,9},{2,10},{3,11},{4,12},{5,13},{6,14},{7,15},{8,0},{9,1},... | collective-permute-start | bytes 1179656 | tf_op jit(solution)/shard_map/ppermute | solution.py:259
  52.7 4.5 %update.4 = (f32[1,512,8192]{2,1,0:T(8,128)}, bf16[512,8192]{1,0:T(8,128)(2,1)}, f32[32,8192]{1,0:T(8,128)}) custom-call(f32[32,32]{1,0:T(8,128)S(1)} %get-tuple-element.25.inverse, bf16[512,128]{1,0:T(8,128)(2,1)S(1)} %get-tuple-element.26.left, ...), custom_call_target="tpu_custom_call", output_to_operand_aliasing={{0}: (7, {}), {1}: (8, {}), {2}: (9, {})} | custom-call | flops 4600000000 | bytes 16099999 | tf_op jit(solution)/shard_map/update/pallas_call | solution.py:226
  57.2 4.5 %update.5 = (f32[1,512,8192]{2,1,0:T(8,128)}, bf16[512,8192]{1,0:T(8,128)(2,1)}, f32[32,8192]{1,0:T(8,128)}) custom-call(f32[32,32]{1,0:T(8,128)S(1)} %get-tuple-element.25.inverse, bf16[512,128]{1,0:T(8,128)(2,1)S(1)} %get-tuple-element.26.left, ...), custom_call_target="tpu_custom_call", output_to_operand_aliasing={{0}: (5, {}), {1}: (6, {}), {2}: (7, {})} | custom-call | flops 4600000000 | bytes 16099999 | tf_op jit(solution)/shard_map/update/pallas_call | solution.py:226
  (26 shorter events, 2.2 us)
Async XLA Ops:
  10.1 1.3 %collective-permute-start = (f32[32,512]{1,0:T(8,128)S(1)}, f32[32,512]{1,0:T(8,128)S(1)}, u32[]{:S(2)}, u32[]{:S(2)}) collective-permute-start(f32[32,512]{1,0:T(8,128)S(1)} %get-tuple-element.20), channel_id=1, source_target_pairs={{0,8},{1,9},{2,10},{3,11},{4,12},{5,13},{6,14},{7,15},{8,0},{9,1},... | collective-permute-start | bytes 196616 | tf_op jit(solution)/shard_map/ppermute | solution.py:259
  11.5 4.6 %collective-permute-start.1 = (f32[32,512]{1,0:T(8,128)S(1)}, f32[32,512]{1,0:T(8,128)S(1)}, u32[]{:S(2)}, u32[]{:S(2)}) collective-permute-start(f32[32,512]{1,0:T(8,128)S(1)} %add.37), channel_id=1, source_target_pairs={{0,16},{1,17},{2,18},{3,19},{4,20},{5,21},{6,22},{7,23},{8,24},{9,... | collective-permute-start | bytes 196616 | tf_op jit(solution)/shard_map/ppermute | solution.py:259
  17.3 2.2 %collective-permute-start.2 = (f32[792,128]{1,0:T(8,128)S(1)}, f32[792,128]{1,0:T(8,128)S(1)}, u32[]{:S(2)}, u32[]{:S(2)}) collective-permute-start(f32[792,128]{1,0:T(8,128)S(1)} %terms.4.earlier), channel_id=1, source_target_pairs={{0,8},{1,9},{2,10},{3,11},{4,12},{5,13},{6,14},{7,15},{8,0},{9,1},... | collective-permute-start | bytes 1216520 | tf_op jit(solution)/shard_map/ppermute | solution.py:259
  19.7 6.1 %collective-permute-start.3 = (f32[264,128]{1,0:T(8,128)S(1)}, f32[264,128]{1,0:T(8,128)S(1)}, u32[]{:S(2)}, u32[]{:S(2)}) collective-permute-start(f32[264,128]{1,0:T(8,128)S(1)} %get-tuple-element.39), channel_id=1, source_target_pairs={{0,17},{1,16},{2,19},{3,18},{4,21},{5,20},{6,23},{7,22},{8,25},{9,... | collective-permute-start | bytes 405512 | tf_op jit(solution)/shard_map/ppermute | solution.py:259
  22.2 6.9 %collective-permute-start.4 = (f32[264,128]{1,0:T(8,128)S(1)}, f32[264,128]{1,0:T(8,128)S(1)}, u32[]{:S(2)}, u32[]{:S(2)}) collective-permute-start(f32[264,128]{1,0:T(8,128)S(1)} %get-tuple-element.37), channel_id=1, source_target_pairs={{0,16},{1,17},{2,18},{3,19},{4,20},{5,21},{6,22},{7,23},{8,24},{9,... | collective-permute-start | bytes 405512 | tf_op jit(solution)/shard_map/ppermute | solution.py:259
  22.4 6.7 %collective-permute-start.5 = (f32[264,128]{1,0:T(8,128)S(1)}, f32[264,128]{1,0:T(8,128)S(1)}, u32[]{:S(2)}, u32[]{:S(2)}) collective-permute-start(f32[264,128]{1,0:T(8,128)S(1)} %get-tuple-element.38), channel_id=1, source_target_pairs={{0,1},{1,0},{2,3},{3,2},{4,5},{5,4},{6,7},{7,6},{8,9},{9,8},{10,11... | collective-permute-start | bytes 405512 | tf_op jit(solution)/shard_map/ppermute | solution.py:259
  26.2 3.0 %collective-permute-start.6 = (f32[264,128]{1,0:T(8,128)S(1)}, f32[264,128]{1,0:T(8,128)S(1)}, u32[]{:S(2)}, u32[]{:S(2)}) collective-permute-start(f32[264,128]{1,0:T(8,128)S(1)} %terms.6.earlier), channel_id=1, source_target_pairs={{0,8},{1,9},{2,10},{3,11},{4,12},{5,13},{6,14},{7,15},{8,0},{9,1},... | collective-permute-start | bytes 405512 | tf_op jit(solution)/shard_map/ppermute | solution.py:259
  29.2 6.4 %collective-permute-start.7 = (f32[264,128]{1,0:T(8,128)S(1)}, f32[264,128]{1,0:T(8,128)S(1)}, u32[]{:S(2)}, u32[]{:S(2)}) collective-permute-start(f32[264,128]{1,0:T(8,128)S(1)} %add_add_fusion), channel_id=1, source_target_pairs={{0,2},{1,3},{2,0},{3,1},{4,6},{5,7},{6,4},{7,5},{8,12},{9,13},{10,... | collective-permute-start | bytes 405512 | tf_op jit(solution)/shard_map/ppermute | solution.py:259
  35.6 3.9 %collective-permute-start.8 = (f32[264,128]{1,0:T(8,128)S(1)}, f32[264,128]{1,0:T(8,128)S(1)}, u32[]{:S(2)}, u32[]{:S(2)}) collective-permute-start(f32[264,128]{1,0:T(8,128)S(1)} %add.44), channel_id=1, source_target_pairs={{0,4},{1,5},{2,6},{3,7},{4,0},{5,1},{6,2},{7,3},{8,10},{9,11},{10,... | collective-permute-start | bytes 405512 | tf_op jit(solution)/shard_map/ppermute | solution.py:259
  39.6 5.8 %collective-permute-start.9 = (f32[264,128]{1,0:T(8,128)S(1)}, f32[264,128]{1,0:T(8,128)S(1)}, u32[]{:S(2)}, u32[]{:S(2)}) collective-permute-start(f32[264,128]{1,0:T(8,128)S(1)} %add.45), channel_id=1, source_target_pairs={{0,8},{1,9},{2,10},{3,11},{4,12},{5,13},{6,14},{7,15},{8,0},{9,1},... | collective-permute-start | bytes 405512 | tf_op jit(solution)/shard_map/ppermute | solution.py:259
  42.6 7.7 %collective-permute-start.10 = (f32[256,128]{1,0:T(8,128)S(1)}, f32[256,128]{1,0:T(8,128)S(1)}, u32[]{:S(2)}, u32[]{:S(2)}) collective-permute-start(f32[256,128]{1,0:T(8,128)S(1)} %slice.22.refs_0_), channel_id=1, source_target_pairs={{0,1},{1,0},{2,3},{3,2},{4,5},{5,4},{6,7},{7,6},{8,9},{9,8},{10,11... | collective-permute-start | bytes 393224 | tf_op jit(solution)/shard_map/ppermute | solution.py:259
  43.9 6.7 %collective-permute-start.11 = (f32[256,128]{1,0:T(8,128)S(1)}, f32[256,128]{1,0:T(8,128)S(1)}, u32[]{:S(2)}, u32[]{:S(2)}) collective-permute-start(f32[256,128]{1,0:T(8,128)S(1)} %slice.22.refs_0_), channel_id=1, source_target_pairs={{0,16},{1,17},{2,18},{3,19},{4,20},{5,21},{6,22},{7,23},{8,24},{9,... | collective-permute-start | bytes 393224 | tf_op jit(solution)/shard_map/ppermute | solution.py:259
  45.3 6.4 %collective-permute-start.12 = (f32[256,128]{1,0:T(8,128)S(1)}, f32[256,128]{1,0:T(8,128)S(1)}, u32[]{:S(2)}, u32[]{:S(2)}) collective-permute-start(f32[256,128]{1,0:T(8,128)S(1)} %slice.22.refs_0_), channel_id=1, source_target_pairs={{0,17},{1,16},{2,19},{3,18},{4,21},{5,20},{6,23},{7,22},{8,25},{9,... | collective-permute-start | bytes 393224 | tf_op jit(solution)/shard_map/ppermute | solution.py:259
  51.7 5.5 %collective-permute-start.13 = (f32[768,128]{1,0:T(8,128)S(1)}, f32[768,128]{1,0:T(8,128)S(1)}, u32[]{:S(2)}, u32[]{:S(2)}) collective-permute-start(f32[768,128]{1,0:T(8,128)S(1)} %maximum_add_fusion), channel_id=1, source_target_pairs={{0,8},{1,9},{2,10},{3,11},{4,12},{5,13},{6,14},{7,15},{8,0},{9,1},... | collective-permute-start | bytes 1179656 | tf_op jit(solution)/shard_map/ppermute | solution.py:259

commit v5 on v4

--- a/solution.py
+++ b/solution.py
@@ -46,10 +46,11 @@
 def correct_kernel(parts, grad, error, qt, high, low, pt, grads, errors, factors, total, sems):
     rows, cols = high.shape
     rank = qt.shape[0]
-    width = cols // parts
+    ends = [512 * n for n in range(1, parts - 1)]
+    ends += [ends[-1] + 256 * n for n in range(1, 5)]
+    spans = [pl.ds(start, end - start) for start, end in zip([0] + ends, ends)]
     takes = []
-    for part in range(parts):
-        columns = pl.ds(part * width, width)
+    for part, columns in enumerate(spans):
         takes.append(
             (
                 pltpu.make_async_copy(error.at[0, :, columns], errors.at[:, columns], sems.at[0, part]),
@@ -60,8 +61,7 @@
         for take in takes[-1]:
             take.start()
     total[...] = jnp.zeros_like(total)
-    for part in range(parts):
-        columns = pl.ds(part * width, width)
+    for part, columns in enumerate(spans):
         for take in takes[part]:
             take.wait()
         hi, lo = two(grads[:, columns].astype(F32) + errors[:, columns])
@@ -91,7 +91,7 @@
             pltpu.VMEM((rows, cols), F32),
             pltpu.VMEM((rank, cols), F32),
             pltpu.VMEM((rank, rows), F32),
-            pltpu.SemaphoreType.DMA((3, parts)),
+            pltpu.SemaphoreType.DMA((3, parts + 2)),
         ],
         compiler_params=params(32),
         name="correct",

time: 62 us -> 61.9 us (level)
  no operation moved by 1% of the time
where the time goes in v5:
time: 61.9 us; the launch traced here: 61.8 us
  Pallas kernels  26.6 us (43%)
  starting transfers between devices  17.8 us (29%)
  waiting for transfers between devices  16.3 us (26%)
  between operations  0.9 us (1%)
    ppermute x14, starting transfers between devices, swap(): lax.ppermute(x, AXES, [(i, i ^ masks[i // CORE & 1]) for i in range(devic...  17.8 us
    ppermute x14, waiting for transfers between devices, swap(): lax.ppermute(x, AXES, [(i, i ^ masks[i // CORE & 1]) for i in range(devic...  16.3 us
    pallas_call x3, Pallas kernels, update_of(): pl.pallas_call(functools.partial(update_kernel, replicas, tuple(spots), l...  12.4 us
    pallas_call x1, Pallas kernels, correct(): pl.pallas_call(functools.partial(correct_kernel, parts), in_specs=[pl.Blo...  9.39 us
    pallas_call x4, Pallas kernels, terms_of(): pl.pallas_call(functools.partial(terms_kernel, replicas, first, paired, w...  3.4 us
    pallas_call x1, Pallas kernels, factor(): pl.pallas_call(functools.partial(factor_kernel, paired), in_specs=[VMEM]...  1.45 us
  transfers between devices with their start and end apart: 14, of which 9 were waited for; matrix products, arithmetic and copies ran while one was open for 0% of the time, Pallas kernels for 19%

profile of v5, /device:TPU:1, one launch (start us, length us, event | category | flops | bytes accessed | tf_op | source)
XLA Modules:
  0.0 61.8 jit_solution(15751168468833654054)
XLA Ops:
  0.6 9.4 %correct.1 = (bf16[512,8192]{1,0:T(8,128)(2,1)S(1)}, bf16[512,8192]{1,0:T(8,128)(2,1)S(1)}, f32[32,512]{1,0:T(8,128)S(1)}) custom-call(bf16[1,512,8192]{2,1,0:T(8,128)(2,1)} %grad.1, f32[1,512,8192]{2,1,0:T(8,128)} %error.1, f32[32,8192]{1,0:T(8,128)} %bitcast.5), custom_call_target="tpu_custom_call" | custom-call | tf_op jit(solution)/shard_map/correct/pallas_call | solution.py:80
  10.2 1.2 %collective-permute-done = f32[32,512]{1,0:T(8,128)S(1)} collective-permute-done((f32[32,512]{1,0:T(8,128)S(1)}, f32[32,512]{1,0:T(8,128)S(1)}, u32[]{:S(2)}, u32[]{:S(2)}) %collective-permute-start) | collective-permute-done | bytes 65568 | tf_op jit(solution)/shard_map/ppermute | solution.py:259
  11.4 2.5 %collective-permute-start.1 = (f32[32,512]{1,0:T(8,128)S(1)}, f32[32,512]{1,0:T(8,128)S(1)}, u32[]{:S(2)}, u32[]{:S(2)}) collective-permute-start(f32[32,512]{1,0:T(8,128)S(1)} %add.37), channel_id=1, source_target_pairs={{0,16},{1,17},{2,18},{3,19},{4,20},{5,21},{6,22},{7,23},{8,24},{9,... | collective-permute-start | bytes 196616 | tf_op jit(solution)/shard_map/ppermute | solution.py:259
  13.8 2.2 %collective-permute-done.1 = f32[32,512]{1,0:T(8,128)S(1)} collective-permute-done((f32[32,512]{1,0:T(8,128)S(1)}, f32[32,512]{1,0:T(8,128)S(1)}, u32[]{:S(2)}, u32[]{:S(2)}) %collective-permute-start.1) | collective-permute-done | bytes 65568 | tf_op jit(solution)/shard_map/ppermute | solution.py:259
  16.0 1.2 %terms.4.earlier = f32[792,128]{1,0:T(8,128)S(1)} custom-call(f32[32,512]{1,0:T(8,128)S(1)} %add.38.pt.earlier, bf16[512,8192]{1,0:T(8,128)(2,1)S(1)} %get-tuple-element.21.high, bf16[512,8192]{1,0:T(8,128)(2,1)S(1)} %get-tuple-element.22.low, f32[32,512]{1,0:T(8,128)S(1)} %add.38.pt.earlier), custom_call_target="tpu_custom_call" | custom-call | flops 1200000000 | bytes 4200000 | tf_op jit(solution)/shard_map/terms/pallas_call | solution.py:131
  17.2 0.9 %collective-permute-start.2 = (f32[792,128]{1,0:T(8,128)S(1)}, f32[792,128]{1,0:T(8,128)S(1)}, u32[]{:S(2)}, u32[]{:S(2)}) collective-permute-start(f32[792,128]{1,0:T(8,128)S(1)} %terms.4.earlier), channel_id=1, source_target_pairs={{0,8},{1,9},{2,10},{3,11},{4,12},{5,13},{6,14},{7,15},{8,0},{9,1},... | collective-permute-start | bytes 1216520 | tf_op jit(solution)/shard_map/ppermute | solution.py:259
  18.1 1.2 %terms.5 = (f32[792,128]{1,0:T(8,128)S(1)}, f32[32,512]{1,0:T(8,128)S(1)}) custom-call(f32[32,512]{1,0:T(8,128)S(1)} %add.38.pt.earlier, bf16[512,8192]{1,0:T(8,128)(2,1)S(1)} %get-tuple-element.21.high, bf16[512,8192]{1,0:T(8,128)(2,1)S(1)} %get-tuple-element.22.low, f32[792,128]{1,0:T(8,128)S(1)} %terms.4.earlier), custom_call_target="tpu_custom_call" | custom-call | flops 1200000000 | bytes 4200000 | tf_op jit(solution)/shard_map/terms/pallas_call | solution.py:131
  19.5 2.6 %collective-permute-start.3 = (f32[264,128]{1,0:T(8,128)S(1)}, f32[264,128]{1,0:T(8,128)S(1)}, u32[]{:S(2)}, u32[]{:S(2)}) collective-permute-start(f32[264,128]{1,0:T(8,128)S(1)} %get-tuple-element.39), channel_id=1, source_target_pairs={{0,17},{1,16},{2,19},{3,18},{4,21},{5,20},{6,23},{7,22},{8,25},{9,... | collective-permute-start | bytes 405512 | tf_op jit(solution)/shard_map/ppermute | solution.py:259
  22.5 3.1 %collective-permute-done.3.earlier = f32[264,128]{1,0:T(8,128)S(1)} collective-permute-done((f32[264,128]{1,0:T(8,128)S(1)}, f32[264,128]{1,0:T(8,128)S(1)}, u32[]{:S(2)}, u32[]{:S(2)}) %collective-permute-start.3) | collective-permute-done | bytes 135200 | tf_op jit(solution)/shard_map/ppermute | solution.py:259
  26.1 1.2 %collective-permute-start.6 = (f32[264,128]{1,0:T(8,128)S(1)}, f32[264,128]{1,0:T(8,128)S(1)}, u32[]{:S(2)}, u32[]{:S(2)}) collective-permute-start(f32[264,128]{1,0:T(8,128)S(1)} %terms.6.earlier), channel_id=1, source_target_pairs={{0,8},{1,9},{2,10},{3,11},{4,12},{5,13},{6,14},{7,15},{8,0},{9,1},... | collective-permute-start | bytes 405512 | tf_op jit(solution)/shard_map/ppermute | solution.py:259
  27.8 1.2 %collective-permute-done.4 = f32[264,128]{1,0:T(8,128)S(1)} collective-permute-done((f32[264,128]{1,0:T(8,128)S(1)}, f32[264,128]{1,0:T(8,128)S(1)}, u32[]{:S(2)}, u32[]{:S(2)}) %collective-permute-start.4) | collective-permute-done | bytes 135200 | tf_op jit(solution)/shard_map/ppermute | solution.py:259
  29.1 2.6 %collective-permute-start.7 = (f32[264,128]{1,0:T(8,128)S(1)}, f32[264,128]{1,0:T(8,128)S(1)}, u32[]{:S(2)}, u32[]{:S(2)}) collective-permute-start(f32[264,128]{1,0:T(8,128)S(1)} %add_add_fusion), channel_id=1, source_target_pairs={{0,2},{1,3},{2,0},{3,1},{4,6},{5,7},{6,4},{7,5},{8,12},{9,13},{10,... | collective-permute-start | bytes 405512 | tf_op jit(solution)/shard_map/ppermute | solution.py:259
  31.7 3.9 %collective-permute-done.7 = f32[264,128]{1,0:T(8,128)S(1)} collective-permute-done((f32[264,128]{1,0:T(8,128)S(1)}, f32[264,128]{1,0:T(8,128)S(1)}, u32[]{:S(2)}, u32[]{:S(2)}) %collective-permute-start.7) | collective-permute-done | bytes 135200 | tf_op jit(solution)/shard_map/ppermute | solution.py:259
  35.5 0.8 %collective-permute-start.8 = (f32[264,128]{1,0:T(8,128)S(1)}, f32[264,128]{1,0:T(8,128)S(1)}, u32[]{:S(2)}, u32[]{:S(2)}) collective-permute-start(f32[264,128]{1,0:T(8,128)S(1)} %add.44), channel_id=1, source_target_pairs={{0,4},{1,5},{2,6},{3,7},{4,0},{5,1},{6,2},{7,3},{8,10},{9,11},{10,... | collective-permute-start | bytes 405512 | tf_op jit(solution)/shard_map/ppermute | solution.py:259
  36.3 3.2 %collective-permute-done.8 = f32[264,128]{1,0:T(8,128)S(1)} collective-permute-done((f32[264,128]{1,0:T(8,128)S(1)}, f32[264,128]{1,0:T(8,128)S(1)}, u32[]{:S(2)}, u32[]{:S(2)}) %collective-permute-start.8) | collective-permute-done | bytes 135200 | tf_op jit(solution)/shard_map/ppermute | solution.py:259
  39.5 3.0 %collective-permute-start.9 = (f32[264,128]{1,0:T(8,128)S(1)}, f32[264,128]{1,0:T(8,128)S(1)}, u32[]{:S(2)}, u32[]{:S(2)}) collective-permute-start(f32[264,128]{1,0:T(8,128)S(1)} %add.45), channel_id=1, source_target_pairs={{0,8},{1,9},{2,10},{3,11},{4,12},{5,13},{6,14},{7,15},{8,0},{9,1},... | collective-permute-start | bytes 405512 | tf_op jit(solution)/shard_map/ppermute | solution.py:259
  42.5 1.3 %collective-permute-start.10 = (f32[256,128]{1,0:T(8,128)S(1)}, f32[256,128]{1,0:T(8,128)S(1)}, u32[]{:S(2)}, u32[]{:S(2)}) collective-permute-start(f32[256,128]{1,0:T(8,128)S(1)} %slice.22.refs_0_), channel_id=1, source_target_pairs={{0,1},{1,0},{2,3},{3,2},{4,5},{5,4},{6,7},{7,6},{8,9},{9,8},{10,11... | collective-permute-start | bytes 393224 | tf_op jit(solution)/shard_map/ppermute | solution.py:259
  43.8 1.4 %collective-permute-start.11 = (f32[256,128]{1,0:T(8,128)S(1)}, f32[256,128]{1,0:T(8,128)S(1)}, u32[]{:S(2)}, u32[]{:S(2)}) collective-permute-start(f32[256,128]{1,0:T(8,128)S(1)} %slice.22.refs_0_), channel_id=1, source_target_pairs={{0,16},{1,17},{2,18},{3,19},{4,20},{5,21},{6,22},{7,23},{8,24},{9,... | collective-permute-start | bytes 393224 | tf_op jit(solution)/shard_map/ppermute | solution.py:259
  45.3 1.4 %factor.1 = (f32[32,32]{1,0:T(8,128)S(1)}, bf16[512,128]{1,0:T(8,128)(2,1)S(1)}) custom-call(f32[8,128]{1,0:T(8,128)S(1)} %slice.20.gram, f32[8,128]{1,0:T(8,128)S(1)} %slice.21.other, f32[32,512]{1,0:T(8,128)S(1)} %get-tuple-element.24.mean), custom_call_target="tpu_custom_call" | custom-call | flops 1500000000 | bytes 5250000 | tf_op jit(solution)/shard_map/factor/pallas_call | solution.py:176
  46.8 3.4 %update.3 = (f32[1,512,8192]{2,1,0:T(8,128)}, bf16[512,8192]{1,0:T(8,128)(2,1)}, f32[32,8192]{1,0:T(8,128)}, f32[8,128]{1,0:T(8,128)S(1)}) custom-call(f32[32,32]{1,0:T(8,128)S(1)} %get-tuple-element.25.inverse, bf16[512,128]{1,0:T(8,128)(2,1)S(1)} %get-tuple-element.26.left, bf16[512,8192]{1,0:T(8,128)(2,1)S(1)} %get-tuple-element.21.high, ...), custom_call_target="tpu_custom_call" | custom-call | flops 3400000000 | bytes 11900000 | tf_op jit(solution)/shard_map/update/pallas_call | solution.py:226
  50.4 1.1 %collective-permute-done.12.refs_2_ = f32[256,128]{1,0:T(8,128)S(1)} collective-permute-done((f32[256,128]{1,0:T(8,128)S(1)}, f32[256,128]{1,0:T(8,128)S(1)}, u32[]{:S(2)}, u32[]{:S(2)}) %collective-permute-start.12) | collective-permute-done | bytes 131104 | tf_op jit(solution)/shard_map/ppermute | solution.py:259
  51.6 1.0 %collective-permute-start.13 = (f32[768,128]{1,0:T(8,128)S(1)}, f32[768,128]{1,0:T(8,128)S(1)}, u32[]{:S(2)}, u32[]{:S(2)}) collective-permute-start(f32[768,128]{1,0:T(8,128)S(1)} %maximum_add_fusion), channel_id=1, source_target_pairs={{0,8},{1,9},{2,10},{3,11},{4,12},{5,13},{6,14},{7,15},{8,0},{9,1},... | collective-permute-start | bytes 1179656 | tf_op jit(solution)/shard_map/ppermute | solution.py:259
  52.6 4.5 %update.4 = (f32[1,512,8192]{2,1,0:T(8,128)}, bf16[512,8192]{1,0:T(8,128)(2,1)}, f32[32,8192]{1,0:T(8,128)}) custom-call(f32[32,32]{1,0:T(8,128)S(1)} %get-tuple-element.25.inverse, bf16[512,128]{1,0:T(8,128)(2,1)S(1)} %get-tuple-element.26.left, ...), custom_call_target="tpu_custom_call", output_to_operand_aliasing={{0}: (7, {}), {1}: (8, {}), {2}: (9, {})} | custom-call | flops 4600000000 | bytes 16099999 | tf_op jit(solution)/shard_map/update/pallas_call | solution.py:226
  57.1 4.5 %update.5 = (f32[1,512,8192]{2,1,0:T(8,128)}, bf16[512,8192]{1,0:T(8,128)(2,1)}, f32[32,8192]{1,0:T(8,128)}) custom-call(f32[32,32]{1,0:T(8,128)S(1)} %get-tuple-element.25.inverse, bf16[512,128]{1,0:T(8,128)(2,1)S(1)} %get-tuple-element.26.left, ...), custom_call_target="tpu_custom_call", output_to_operand_aliasing={{0}: (5, {}), {1}: (6, {}), {2}: (7, {})} | custom-call | flops 4600000000 | bytes 16099999 | tf_op jit(solution)/shard_map/update/pallas_call | solution.py:226
  (26 shorter events, 2.2 us)
Async XLA Ops:
  10.0 1.3 %collective-permute-start = (f32[32,512]{1,0:T(8,128)S(1)}, f32[32,512]{1,0:T(8,128)S(1)}, u32[]{:S(2)}, u32[]{:S(2)}) collective-permute-start(f32[32,512]{1,0:T(8,128)S(1)} %get-tuple-element.20), channel_id=1, source_target_pairs={{0,8},{1,9},{2,10},{3,11},{4,12},{5,13},{6,14},{7,15},{8,0},{9,1},... | collective-permute-start | bytes 196616 | tf_op jit(solution)/shard_map/ppermute | solution.py:259
  11.4 4.6 %collective-permute-start.1 = (f32[32,512]{1,0:T(8,128)S(1)}, f32[32,512]{1,0:T(8,128)S(1)}, u32[]{:S(2)}, u32[]{:S(2)}) collective-permute-start(f32[32,512]{1,0:T(8,128)S(1)} %add.37), channel_id=1, source_target_pairs={{0,16},{1,17},{2,18},{3,19},{4,20},{5,21},{6,22},{7,23},{8,24},{9,... | collective-permute-start | bytes 196616 | tf_op jit(solution)/shard_map/ppermute | solution.py:259
  17.2 2.2 %collective-permute-start.2 = (f32[792,128]{1,0:T(8,128)S(1)}, f32[792,128]{1,0:T(8,128)S(1)}, u32[]{:S(2)}, u32[]{:S(2)}) collective-permute-start(f32[792,128]{1,0:T(8,128)S(1)} %terms.4.earlier), channel_id=1, source_target_pairs={{0,8},{1,9},{2,10},{3,11},{4,12},{5,13},{6,14},{7,15},{8,0},{9,1},... | collective-permute-start | bytes 1216520 | tf_op jit(solution)/shard_map/ppermute | solution.py:259
  19.5 6.1 %collective-permute-start.3 = (f32[264,128]{1,0:T(8,128)S(1)}, f32[264,128]{1,0:T(8,128)S(1)}, u32[]{:S(2)}, u32[]{:S(2)}) collective-permute-start(f32[264,128]{1,0:T(8,128)S(1)} %get-tuple-element.39), channel_id=1, source_target_pairs={{0,17},{1,16},{2,19},{3,18},{4,21},{5,20},{6,23},{7,22},{8,25},{9,... | collective-permute-start | bytes 405512 | tf_op jit(solution)/shard_map/ppermute | solution.py:259
  22.1 6.9 %collective-permute-start.4 = (f32[264,128]{1,0:T(8,128)S(1)}, f32[264,128]{1,0:T(8,128)S(1)}, u32[]{:S(2)}, u32[]{:S(2)}) collective-permute-start(f32[264,128]{1,0:T(8,128)S(1)} %get-tuple-element.37), channel_id=1, source_target_pairs={{0,16},{1,17},{2,18},{3,19},{4,20},{5,21},{6,22},{7,23},{8,24},{9,... | collective-permute-start | bytes 405512 | tf_op jit(solution)/shard_map/ppermute | solution.py:259
  22.3 6.7 %collective-permute-start.5 = (f32[264,128]{1,0:T(8,128)S(1)}, f32[264,128]{1,0:T(8,128)S(1)}, u32[]{:S(2)}, u32[]{:S(2)}) collective-permute-start(f32[264,128]{1,0:T(8,128)S(1)} %get-tuple-element.38), channel_id=1, source_target_pairs={{0,1},{1,0},{2,3},{3,2},{4,5},{5,4},{6,7},{7,6},{8,9},{9,8},{10,11... | collective-permute-start | bytes 405512 | tf_op jit(solution)/shard_map/ppermute | solution.py:259
  26.1 3.0 %collective-permute-start.6 = (f32[264,128]{1,0:T(8,128)S(1)}, f32[264,128]{1,0:T(8,128)S(1)}, u32[]{:S(2)}, u32[]{:S(2)}) collective-permute-start(f32[264,128]{1,0:T(8,128)S(1)} %terms.6.earlier), channel_id=1, source_target_pairs={{0,8},{1,9},{2,10},{3,11},{4,12},{5,13},{6,14},{7,15},{8,0},{9,1},... | collective-permute-start | bytes 405512 | tf_op jit(solution)/shard_map/ppermute | solution.py:259
  29.1 6.4 %collective-permute-start.7 = (f32[264,128]{1,0:T(8,128)S(1)}, f32[264,128]{1,0:T(8,128)S(1)}, u32[]{:S(2)}, u32[]{:S(2)}) collective-permute-start(f32[264,128]{1,0:T(8,128)S(1)} %add_add_fusion), channel_id=1, source_target_pairs={{0,2},{1,3},{2,0},{3,1},{4,6},{5,7},{6,4},{7,5},{8,12},{9,13},{10,... | collective-permute-start | bytes 405512 | tf_op jit(solution)/shard_map/ppermute | solution.py:259
  35.5 3.9 %collective-permute-start.8 = (f32[264,128]{1,0:T(8,128)S(1)}, f32[264,128]{1,0:T(8,128)S(1)}, u32[]{:S(2)}, u32[]{:S(2)}) collective-permute-start(f32[264,128]{1,0:T(8,128)S(1)} %add.44), channel_id=1, source_target_pairs={{0,4},{1,5},{2,6},{3,7},{4,0},{5,1},{6,2},{7,3},{8,10},{9,11},{10,... | collective-permute-start | bytes 405512 | tf_op jit(solution)/shard_map/ppermute | solution.py:259
  39.5 5.8 %collective-permute-start.9 = (f32[264,128]{1,0:T(8,128)S(1)}, f32[264,128]{1,0:T(8,128)S(1)}, u32[]{:S(2)}, u32[]{:S(2)}) collective-permute-start(f32[264,128]{1,0:T(8,128)S(1)} %add.45), channel_id=1, source_target_pairs={{0,8},{1,9},{2,10},{3,11},{4,12},{5,13},{6,14},{7,15},{8,0},{9,1},... | collective-permute-start | bytes 405512 | tf_op jit(solution)/shard_map/ppermute | solution.py:259
  42.5 7.7 %collective-permute-start.10 = (f32[256,128]{1,0:T(8,128)S(1)}, f32[256,128]{1,0:T(8,128)S(1)}, u32[]{:S(2)}, u32[]{:S(2)}) collective-permute-start(f32[256,128]{1,0:T(8,128)S(1)} %slice.22.refs_0_), channel_id=1, source_target_pairs={{0,1},{1,0},{2,3},{3,2},{4,5},{5,4},{6,7},{7,6},{8,9},{9,8},{10,11... | collective-permute-start | bytes 393224 | tf_op jit(solution)/shard_map/ppermute | solution.py:259
  43.8 6.7 %collective-permute-start.11 = (f32[256,128]{1,0:T(8,128)S(1)}, f32[256,128]{1,0:T(8,128)S(1)}, u32[]{:S(2)}, u32[]{:S(2)}) collective-permute-start(f32[256,128]{1,0:T(8,128)S(1)} %slice.22.refs_0_), channel_id=1, source_target_pairs={{0,16},{1,17},{2,18},{3,19},{4,20},{5,21},{6,22},{7,23},{8,24},{9,... | collective-permute-start | bytes 393224 | tf_op jit(solution)/shard_map/ppermute | solution.py:259
  45.2 6.4 %collective-permute-start.12 = (f32[256,128]{1,0:T(8,128)S(1)}, f32[256,128]{1,0:T(8,128)S(1)}, u32[]{:S(2)}, u32[]{:S(2)}) collective-permute-start(f32[256,128]{1,0:T(8,128)S(1)} %slice.22.refs_0_), channel_id=1, source_target_pairs={{0,17},{1,16},{2,19},{3,18},{4,21},{5,20},{6,23},{7,22},{8,25},{9,... | collective-permute-start | bytes 393224 | tf_op jit(solution)/shard_map/ppermute | solution.py:259
  51.6 5.5 %collective-permute-start.13 = (f32[768,128]{1,0:T(8,128)S(1)}, f32[768,128]{1,0:T(8,128)S(1)}, u32[]{:S(2)}, u32[]{:S(2)}) collective-permute-start(f32[768,128]{1,0:T(8,128)S(1)} %maximum_add_fusion), channel_id=1, source_target_pairs={{0,8},{1,9},{2,10},{3,11},{4,12},{5,13},{6,14},{7,15},{8,0},{9,1},... | collective-permute-start | bytes 1179656 | tf_op jit(solution)/shard_map/ppermute | solution.py:259
